TPU v7x, 256 devices: a whole 4x4x8 slice. The times are simulated.
256 devices in a mesh: seq: 32 (over z, y), tensor: 8 (over x, core).
Axes of the slice: x: 4, y: 4, z: 8, core: 2. Of those that a mesh axis runs over, the one named last changes fastest.
Arguments:
- projections: bfloat16 [3, 8192, 8192], P(None, 'seq', 'tensor'), may hold values from -6 to 6
- out_grad: bfloat16 [8192, 8192], P('seq', 'tensor'), may hold values from -6 to 6
- short_filters: float32 [3, 7, 8192], P(None, None, 'tensor'), may hold values from -2 to 2
- long_filter: float32 [128, 8192], P('seq', 'tensor'), may hold values from -0.5 to 0.5
Outputs:
- grad_projections: bfloat16 [3, 8192, 8192], P(None, 'seq', 'tensor')
- grad_short: float32 [3, 7, 8192], P(None, None, 'tensor')
- grad_long: float32 [128, 8192], P('seq', 'tensor')
All inputs are finite; a program needn't handle non-finite values.
Results may differ from a plain program's by a relative error of at most 0.006.
Values may be sent and summed in bfloat16 or wider, within the bound.
A program may use at most 64 MiB of HBM per device.

v0:
```python
import jax
import jax.numpy as jnp
from jax import lax
from jax.sharding import PartitionSpec as P

STAPS = 7
LTAPS = 128


def passed_along(block, axis, distance):
    devices = range(lax.axis_size(axis))
    route = [(i - distance, i) for i in devices if i - distance in devices]
    return lax.ppermute(block, axis, route)


def shortened(shard):
    return jax.tree.map(lambda a: a.astype(jnp.bfloat16) if a.dtype == jnp.float32 else a, shard)


def correlate(extended, taps):
    result = lax.conv_general_dilated(
        extended[None],
        taps[:, None, :],
        (1,),
        "VALID",
        dimension_numbers=("NWC", "WIO", "NWC"),
        feature_group_count=extended.shape[1],
        precision=lax.Precision.HIGHEST,
    )
    return result[0]


def on_device(projections, out_grad, short_filters, long_filter):
    row_count = projections.shape[1]
    full_taps = lax.all_gather(long_filter, "seq", axis=0, tiled=True)
    earlier = passed_along(projections[:, row_count - (STAPS - 1) :, :], "seq", 1)
    inputs_ext = jnp.concatenate([earlier, projections], axis=1).astype(jnp.float32)
    features = jax.vmap(correlate)(inputs_ext, short_filters[:, ::-1])
    gating = features[1] * features[2]
    prior_gating = passed_along(shortened(gating[row_count - (LTAPS - 1) :]), "seq", 1)
    history = jnp.concatenate([prior_gating, gating], axis=0)
    cotangent = out_grad.astype(jnp.float32)
    mixing = correlate(history, full_taps[::-1])
    grad_query = cotangent * mixing
    grad_mixing = cotangent * features[0]
    later_mixing = passed_along(shortened(grad_mixing[: LTAPS - 1]), "seq", -1)
    grad_gating = correlate(jnp.concatenate([grad_mixing, later_mixing], axis=0), full_taps)
    grad_features = jnp.stack([grad_query, grad_gating * features[2], grad_gating * features[1]])
    later_features = passed_along(shortened(grad_features[:, : STAPS - 1]), "seq", -1)
    grad_inputs = jax.vmap(correlate)(
        jnp.concatenate([grad_features, later_features], axis=1), short_filters
    ).astype(jnp.bfloat16)
    partial_short = jax.vmap(correlate)(inputs_ext, grad_features)[:, ::-1]
    partial_long = correlate(history, grad_mixing)[::-1]
    grad_long = lax.psum_scatter(partial_long, "seq", scatter_dimension=0, tiled=True)
    grad_short = lax.psum(partial_short, "seq")
    return (grad_inputs, grad_short, grad_long)


def solution(mesh):
    in_specs = (
        P(None, "seq", "tensor"),
        P("seq", "tensor"),
        P(None, None, "tensor"),
        P("seq", "tensor"),
    )
    out_specs = (P(None, "seq", "tensor"), P(None, None, "tensor"), P("seq", "tensor"))
    return jax.shard_map(
        on_device, mesh=mesh, in_specs=in_specs, out_specs=out_specs, check_vma=False
    )
```

profile of v0, /device:TPU:2, one launch (start us, length us, event | category | flops | bytes accessed | tf_op | source)
XLA Modules:
  0.0 339.5 jit_solution(2204245202897858139)
XLA Ops:
  7.2 0.9 slice.30
  8.2 3.5 %collective-permute-start = (bf16[3,6,1024]{2,1,0:T(8,128)(2,1)S(1)}, bf16[3,6,1024]{2,1,0:T(8,128)(2,1)S(1)}, u32[]{:S(2)}, u32[]{:S(2)}) collective-permute-start(bf16[3,6,1024]{2,1,0:T(8,128)(2,1)S(1)} %slice.30), channel_id=1, source_target_pairs={{0,8},{8,16},{16,24},{24,32},{32,40},{40,48},{48,56},{56,64},{64,7... | collective-permute-start | bytes 110600 | tf_op jit(solution)/shard_map/ppermute | solution.py:13
  11.7 52.2 %all-gather = f32[32,4,1024]{2,1,0:T(4,128)S(1)} all-gather(f32[1,4,1024]{2,1,0:T(4,128)} %bitcast.82), channel_id=1, replica_groups=mesh['seq'=32,'tensor'=8] {'seq'}, dimensions={0}, use_global_device_ids=true | all-gather | bytes 540672 | tf_op jit(solution)/shard_map/all_gather | solution.py:35
  63.9 1.6 broadcast_in_dim.37
  65.4 0.2 reshape.91
  65.6 2.9 rev.12
  68.6 0.1 reshape.61
  68.8 0.8 reshape.66
  69.6 0.2 rev.13
  69.8 1.2 broadcast_in_dim.35
  71.0 0.6 dynamic-slice
  72.2 0.4 maximum_bitcast_fusion.1
  72.7 1.4 copy.35
  74.1 3.3 reshape.59
  77.4 2.7 pad
  80.1 2.0 reshape.72
  82.1 0.9 copy.37
  83.0 0.1 slice.41
  83.1 1.7 convolution_select_fusion
  84.8 3.8 %copy.39 = f32[8,33,3072]{2,1,0:T(8,128)} copy(f32[8,33,3072]{2,0,1:T(8,128)S(1)} %convolution_select_fusion) | data formatting | bytes 6488064 | tf_op jit(solution)/shard_map/vmap()/conv_general_dilated | solution.py:21
  88.5 2.5 reshape.76
  91.1 1.9 slice.42
  92.9 3.6 %copy.40 = f32[1,256,3072]{1,2,0:T(8,128)} copy(f32[1,256,3072]{2,1,0:T(8,128)} %slice.42) | data formatting | bytes 6291456 | tf_op jit(solution)/shard_map/vmap()/conv_general_dilated | solution.py:21
  96.5 2.6 copy.41
  99.1 0.2 slice_multiply_fusion
  99.3 3.3 collective-permute-start.1
  102.6 0.2 fusion.47
  102.8 3.7 %collective-permute-done.1 = bf16[127,1024]{1,0:T(8,128)(2,1)S(1)} collective-permute-done((bf16[127,1024]{1,0:T(8,128)(2,1)S(1)}, bf16[127,1024]{1,0:T(8,128)(2,1)S(1)}, u32[]{:S(2)}, u32[]{:S(2)}) %collective-permute-start.1) | collective-permute-done | bytes 260128 | tf_op jit(solution)/shard_map/ppermute | solution.py:13
  106.6 0.2 pad_maximum_fusion.1
  106.8 1.1 broadcast_in_dim.34
  107.9 14.5 %fusion.39 = f32[1,256,1024]{2,0,1:T(1,128)S(1)} fusion(f32[1,383,1024]{2,0,1:T(1,128)S(1)} %broadcast_in_dim.34, f32[128,1,1024]{2,1,0:T(1,128)S(1)} %copy-done.7), kind=kOutput, calls=%fused_computation.50 | convolution fusion | flops 402653184 | bytes 3141632 | tf_op jit(solution)/shard_map/conv_general_dilated | solution.py:21
  122.4 1.4 fusion.27
  123.8 1.3 collective-permute-start.2
  125.1 10.5 %fusion.28 = f32[1,128,1024]{2,0,1:T(1,128)S(1)} fusion(f32[1,383,1024]{2,0,1:T(1,128)S(1)} %broadcast_in_dim.34, f32[256,1,1024]{2,0,1:T(8,128)S(1)} %bitcast.77), kind=kOutput, calls=%fused_computation.33 | convolution fusion | flops 402653184 | bytes 3141632 | tf_op jit(solution)/shard_map/conv_general_dilated | solution.py:21
  135.6 0.1 copy.71
  135.7 2.7 rev.15
  138.5 1.3 maximum_bitcast_fusion.2
  139.8 10.6 %fusion.22 = f32[1,256,1024]{2,0,1:T(1,128)S(1)} fusion(f32[128,1,1024]{2,1,0:T(1,128)S(1)} %copy-done.6, f32[1,383,1024]{2,1,0:T(8,128)S(1)} %maximum_bitcast_fusion.2), kind=kOutput, calls=%fused_computation.24 | convolution fusion | flops 402653184 | bytes 3141632 | tf_op jit(solution)/shard_map/conv_general_dilated | solution.py:21
  150.4 0.4 bitcast_multiply_fusion.1
  150.8 0.8 copy-done.2
  151.6 0.3 pad_maximum_fusion
  152.0 1.9 fusion.38
  153.9 1.3 collective-permute-start.3
  155.2 3.7 %copy.51 = f32[256,1,3,1024]{0,3,2,1:T(8,128)} copy(f32[256,1,3,1024]{3,0,2,1:T(8,128)} %fusion.38) | data formatting | bytes 6291456 | tf_op jit(solution)/shard_map/vmap()/reshape | solution.py:21
  158.9 7.7 %copy.53 = f32[256,1,3072]{2,1,0:T(1,128)} copy(f32[256,1,3072]{0,2,1:T(8,128)} %bitcast.75) | data formatting | bytes 6291456 | tf_op jit(solution)/shard_map/vmap()/reshape | solution.py:21
  166.7 8.0 %fusion.24 = f32[7,3072]{1,0:T(8,128)S(1)} fusion(f32[256,1,3072]{2,1,0:T(1,128)} %copy.53, bf16[1,262,3072]{2,1,0:T(8,128)(2,1)} %reshape.59), kind=kOutput, calls=%fused_computation.28 | convolution fusion | flops 66060288 | bytes 4841472 | tf_op jit(solution)/shard_map/vmap()/conv_general_dilated | solution.py:21
  174.6 0.1 reshape.69
  174.7 0.7 rev.14
  175.4 0.2 maximum_bitcast_fusion
  175.7 4.2 %copy.45 = f32[1,262,3,1024]{3,2,1,0:T(4,128)} copy(f32[1,262,3,1024]{3,1,2,0:T(8,128)S(1)} %maximum_bitcast_fusion) | data formatting | bytes 6438912 | tf_op jit(solution)/shard_map/vmap()/reshape | solution.py:21
  179.8 5.0 %reshape.64 = f32[1,262,3072]{2,1,0:T(8,128)S(1)} reshape(f32[1,262,3,1024]{3,2,1,0:T(4,128)} %copy.45) | data formatting | bytes 6438912 | tf_op jit(solution)/shard_map/vmap()/reshape | solution.py:21
  184.9 1.9 pad.2
  186.8 5.1 %reshape.79 = f32[1,8,33,3072]{3,0,2,1:T(1,128)S(1)} reshape(f32[1,264,3072]{2,1,0:T(8,128)} %pad.2) | data formatting | bytes 6488064 | tf_op jit(solution)/shard_map/vmap()/conv_general_dilated | solution.py:21
  191.9 0.6 copy.47
  192.6 0.2 copy-done.9
  192.8 2.9 fusion.9
  195.7 0.9 copy.49
  196.6 1.7 reshape.83
  198.3 1.4 slice-done
  199.7 0.7 copy.50
  200.4 1.7 copy.55
  202.2 127.5 %all-reduce.4.cloned.1.call-done = (f32[3,7,1024]{2,0,1:T(4,128)}, f32[128,1024]{1,0:T(8,128)}) async-done(((f32[3,7,1024]{2,0,1:T(4,128)}, f32[128,1024]{1,0:T(8,128)}), (f32[3,7,1024]{2,0,1:T(4,128)}, f32[128,1024]{1,0:T(8,128)})) %all-reduce.4.cloned.1.call-update) | async-done | bytes 610320 | tf_op jit(solution)/shard_map/psum | solution.py:56
  329.7 1.6 copy.56
  331.3 1.4 constant_dynamic-slice_fusion
  (39 shorter events, 0.5 us)
Async XLA Ops:
  7.2 63.8 %copy-start.10 = (u32[256]{0:T(256)S(1)}, u32[256]{0:T(256)}, u32[]{:S(2)}) copy-start(u32[256]{0:T(256)} %constant.25) | copy-start | bytes 3076
  7.2 65.0 %copy-start.4 = (bf16[3,256,1024]{2,1,0:T(8,128)(2,1)S(1)}, bf16[3,256,1024]{2,1,0:T(8,128)(2,1)}, u32[]{:S(2)}) copy-start(bf16[3,256,1024]{2,1,0:T(8,128)(2,1)} %param.4) | copy-start | bytes 4718596
  7.2 61.5 %copy-start.8 = (f32[3,7,1024]{2,1,0:T(8,128)S(1)}, f32[3,7,1024]{2,1,0:T(8,128)}, u32[]{:S(2)}) copy-start(f32[3,7,1024]{2,1,0:T(8,128)} %param.6) | copy-start | bytes 258052
  7.2 322.5 %all-reduce.4.cloned.1.call-start = ((), (), s32[]{:S(2)}) async-start(), calls=%async_computation | async-start | bytes 1277952 | tf_op jit(solution)/shard_map/psum | solution.py:56
  8.2 64.0 %collective-permute-start = (bf16[3,6,1024]{2,1,0:T(8,128)(2,1)S(1)}, bf16[3,6,1024]{2,1,0:T(8,128)(2,1)S(1)}, u32[]{:S(2)}, u32[]{:S(2)}) collective-permute-start(bf16[3,6,1024]{2,1,0:T(8,128)(2,1)S(1)} %slice.30), channel_id=1, source_target_pairs={{0,8},{8,16},{16,24},{24,32},{32,40},{40,48},{48,56},{56,64},{64,7... | collective-permute-start | bytes 110600 | tf_op jit(solution)/shard_map/ppermute | solution.py:13
  80.1 3.0 copy-start.11
  99.1 23.3 %copy-start = (f32[1,256,3,1024]{3,1,0,2:T(8,128)}, f32[1,256,3,1024]{3,1,0,2:T(8,128)S(1)}, u32[]{:S(2)}) copy-start(f32[1,256,3,1024]{3,1,0,2:T(8,128)S(1)} %copy.41) | copy-start | bytes 9437188
  99.3 7.2 %collective-permute-start.1 = (bf16[127,1024]{1,0:T(8,128)(2,1)S(1)}, bf16[127,1024]{1,0:T(8,128)(2,1)S(1)}, u32[]{:S(2)}, u32[]{:S(2)}) collective-permute-start(bf16[127,1024]{1,0:T(8,128)(2,1)S(1)} %fusion.31), channel_id=1, source_target_pairs={{0,8},{8,16},{16,24},{24,32},{32,40},{40,48},{48,56},{56,64},{64,7... | collective-permute-start | bytes 780296 | tf_op jit(solution)/shard_map/ppermute | solution.py:13
  106.6 1.3 copy-start.7
  107.9 14.5 %copy-start.5 = (bf16[256,1024]{1,0:T(8,128)(2,1)S(1)}, bf16[256,1024]{1,0:T(8,128)(2,1)}, u32[]{:S(2)}) copy-start(bf16[256,1024]{1,0:T(8,128)(2,1)} %param.5) | copy-start | bytes 1572868
  123.8 11.9 %copy-start.3 = (f32[256,1024]{1,0:T(8,128)}, f32[256,1024]{1,0:T(8,128)S(1)}, u32[]{:S(2)}) copy-start(f32[256,1024]{1,0:T(8,128)S(1)} %get-tuple-element.14) | copy-start | bytes 3145732
  123.8 14.6 %collective-permute-start.2 = (bf16[127,1024]{1,0:T(8,128)(2,1)S(1)}, bf16[127,1024]{1,0:T(8,128)(2,1)S(1)}, u32[]{:S(2)}, u32[]{:S(2)}) collective-permute-start(bf16[127,1024]{1,0:T(8,128)(2,1)S(1)} %slice.63), channel_id=1, source_target_pairs={{8,0},{16,8},{24,16},{32,24},{40,32},{48,40},{56,48},{64,56},{72,6... | collective-permute-start | bytes 780296 | tf_op jit(solution)/shard_map/ppermute | solution.py:13
  135.6 4.2 %copy-start.6 = (f32[128,1,1024]{2,1,0:T(1,128)S(1)}, f32[128,1,1024]{2,1,0:T(1,128)}, u32[]{:S(2)}) copy-start(f32[128,1,1024]{2,1,0:T(1,128)} %broadcast_in_dim.37) | copy-start | bytes 1572868
  139.8 10.6 %copy-start.1 = (f32[1,256,3,1024]{3,1,0,2:T(8,128)S(1)}, f32[1,256,3,1024]{3,1,0,2:T(8,128)}, u32[]{:S(2)}) copy-start(f32[1,256,3,1024]{3,1,0,2:T(8,128)} %copy-done) | copy-start | bytes 9437188
  150.4 1.2 copy-start.2
  153.9 21.5 %collective-permute-start.3 = (bf16[3,6,1024]{2,1,0:T(8,128)(2,1)S(1)}, bf16[3,6,1024]{2,1,0:T(8,128)(2,1)S(1)}, u32[]{:S(2)}, u32[]{:S(2)}) collective-permute-start(bf16[3,6,1024]{2,1,0:T(8,128)(2,1)S(1)} %slice.64), channel_id=1, source_target_pairs={{8,0},{16,8},{24,16},{32,24},{40,32},{48,40},{56,48},{64,56},{72,6... | collective-permute-start | bytes 110600 | tf_op jit(solution)/shard_map/ppermute | solution.py:13
  191.9 0.9 copy-start.9
  191.9 0.9 copy-start.12
  198.3 1.4 slice-start
Sparse Core Ops, SparseCore 0:
  175.5 154.1 all-reduce.3
where the time goes:
time: 341 us; the launch traced here: 339 us
  waiting for transfers between devices  131 us (38%)
  local copies, waits for them, and re-layouts  76.7 us (22%)
  blocking collectives  52.2 us (15%)
  matrix products  48.1 us (14%)
  between operations  15.2 us (4%)
  starting transfers between devices  9.41 us (3%)
  other arithmetic  6.7 us (2%)
    psum x1, waiting for transfers between devices, on_device(): grad_short = lax.psum(partial_short, 'seq')  128 us
    all_gather x1, blocking collectives, on_device(): full_taps = lax.all_gather(long_filter, 'seq', axis=0, tiled=True)  52.2 us
    conv_general_dilated x6, matrix products, correlate(): lax.conv_general_dilated(extended[None], taps[:, None, :], (1,), 'VALID',...  48.1 us
    reshape x14, local copies, waits for them, and re-layouts, correlate(): lax.conv_general_dilated(extended[None], taps[:, None, :], (1,), 'VALID',...  33.6 us
    conv_general_dilated x10, local copies, waits for them, and re-layouts, correlate(): lax.conv_general_dilated(extended[None], taps[:, None, :], (1,), 'VALID',...  20.5 us
    ppermute x4, starting transfers between devices, passed_along(): return lax.ppermute(block, axis, route)  9.37 us
  transfers between devices with their start and end apart: 5, of which 2 were waited for; matrix products, arithmetic and copies ran while one was open for 20% of the time, Pallas kernels for 0%

commit v1 on v0

v1 whole, which is shorter than its diff:
```python
import jax
import jax.numpy as jnp
import ml_dtypes
import numpy as np
from jax import lax
from jax.experimental import pallas as pl
from jax.experimental.pallas import tpu as pltpu
from jax.sharding import PartitionSpec as P

MESH = pl.DeviceIdType.MESH
F32 = jnp.float32
BF16 = jnp.bfloat16

STAPS = 7
LTAPS = 128
ROWS = 256
COLS = 1024
LANES = 128
CHUNKS = COLS // LANES
WIDE = 256
QUADS = COLS // WIDE
SEQ = 32
OWN_TAPS = LTAPS // SEQ
POINTS = ROWS + LTAPS
HALF = POINTS // 2
EDGE = 16
PIECES = 3 * CHUNKS


def transforms():
    freqs = 2.0 * np.pi * (np.arange(HALF) + 0.5) / POINTS

    def rows(times):
        angles = np.outer(freqs, times)
        return np.concatenate([np.cos(angles), np.sin(angles)], axis=0)

    own = rows(np.arange(ROWS))
    prior = rows(np.arange(-LTAPS, 0))
    tap_order = np.arange(LTAPS).reshape(SEQ, OWN_TAPS).T.reshape(-1)
    taps = rows(tap_order)
    forward = np.concatenate([own, prior, taps], axis=1).astype(ml_dtypes.bfloat16)
    inverse = np.concatenate([own.T, taps.T], axis=0).astype(ml_dtypes.bfloat16)
    return forward, inverse


def lanes(c):
    return pl.ds(pl.multiple_of(c * LANES, LANES), LANES)


def wide(q):
    return pl.ds(pl.multiple_of(q * WIDE, WIDE), WIDE)


def dot(a, b):
    return jnp.dot(a, b, preferred_element_type=F32)


def kernel(
    proj_hbm, og_hbm, sf_hbm, lf_hbm, fw_hbm, iv_hbm,
    gp_hbm, gs_out, gl_out,
    pv, ov, sfv, lfv, fw, iv,
    xs, fs, fkv, gx, gmx, ph, gfh_send, gfh_recv,
    filt_stage, filt, fperm, spec_g, spec_gm, spec_h, y1, y2, y3,
    lperm, gl_send, gl_recv, gl_sum, gs_part, gs_recv, gs_all, gp_v,
    load_sem, store_sem, ph_sem, g_sem, gm_sem, gm0_sem, gf_sem,
    fsend, frecv, lsend, lrecv, ssend, srecv, asend, arecv,
):
    me = lax.axis_index("seq")
    right, left = lax.rem(me + 1, SEQ), lax.rem(me + SEQ - 1, SEQ)
    has_left, has_right = me > 0, me < SEQ - 1

    def peer(i):
        return lax.rem(me + i, SEQ)

    def remote(src, dst, send_sem, recv_sem, to):
        return pltpu.make_async_remote_copy(
            src_ref=src, dst_ref=dst, send_sem=send_sem, recv_sem=recv_sem,
            device_id={"seq": to}, device_id_type=MESH,
        )

    def loop(low, high, body):
        lax.fori_loop(low, high, lambda i, _: (body(i), 0)[1], 0)

    barrier = pltpu.get_barrier_semaphore()
    loop(1, SEQ, lambda i: pl.semaphore_signal(barrier, inc=1, device_id={"seq": peer(i)}, device_id_type=MESH))

    loads = [
        pltpu.make_async_copy(src, dst, load_sem.at[n])
        for n, (src, dst) in enumerate(
            [
                (sf_hbm, sfv), (proj_hbm.at[1], pv.at[1]), (proj_hbm.at[2], pv.at[2]), (proj_hbm.at[0], pv.at[0]),
                (og_hbm, ov), (lf_hbm, lfv), (fw_hbm, fw), (iv_hbm, iv),
            ]
        )
    ]
    for load in loads:
        load.start()

    def feature(s, c, first, count):
        total = None
        for j in range(STAPS):
            term = sfv[s, j : j + 1, lanes(c)] * xs[s, c, pl.ds(EDGE + first - j, count), :]
            total = term if total is None else total + term
        return total

    def gated(c, first, count):
        k, v = feature(1, c, first, count), feature(2, c, first, count)
        fkv[0, c, pl.ds(first, count), :] = k
        fkv[1, c, pl.ds(first, count), :] = v
        gx[pl.ds(LTAPS + first, count), lanes(c)] = (k * v).astype(BF16)

    def mixed(c, first, count):
        cotangent = ov[pl.ds(first, count), lanes(c)].astype(F32)
        gmx[pl.ds(first, count), lanes(c)] = (cotangent * feature(0, c, first, count)).astype(BF16)

    def widen(s, c):
        xs[s, c, pl.ds(EDGE, ROWS), :] = pv[s, :, lanes(c)].astype(F32)

    for load in loads[:3]:
        load.wait()

    def tail(c):
        widen(1, c)
        widen(2, c)
        for first in (128, 192):
            gated(c, first, 64)

    loop(0, CHUNKS, tail)
    loads[3].wait()
    loads[4].wait()

    def head(c):
        widen(0, c)
        for first, count in ((16, 48), (64, 64)):
            mixed(c, first, count)

    loop(0, CHUNKS, head)
    loads[5].wait()
    for q in range(QUADS):
        lperm[0, OWN_TAPS * q : OWN_TAPS * (q + 1), :] = lfv[:, WIDE * q : WIDE * q + LANES]
        lperm[1, OWN_TAPS * q : OWN_TAPS * (q + 1), :] = lfv[:, WIDE * q + LANES : WIDE * (q + 1)]
    filt_stage[:, 0:LANES] = lperm[0, 0:16, :].astype(BF16)
    filt_stage[:, LANES:WIDE] = lperm[1, 0:16, :].astype(BF16)

    pl.semaphore_wait(barrier, SEQ - 1)

    def ph_copy():
        return remote(pv.at[:, pl.ds(ROWS - EDGE, EDGE), :], ph, ph_sem.at[0], ph_sem.at[1], right)

    def g_copy(q):
        return remote(gx.at[pl.ds(ROWS, LTAPS), wide(q)], gx.at[pl.ds(0, LTAPS), wide(q)], g_sem.at[0, q], g_sem.at[1, q], right)

    def gm_copy(q):
        return remote(
            gmx.at[pl.ds(EDGE, LTAPS - EDGE), wide(q)], gmx.at[pl.ds(ROWS + EDGE, LTAPS - EDGE), wide(q)],
            gm_sem.at[0, q], gm_sem.at[1, q], left,
        )

    def gm0_copy():
        return remote(gmx.at[pl.ds(0, EDGE), :], gmx.at[pl.ds(ROWS, EDGE), :], gm0_sem.at[0], gm0_sem.at[1], left)

    def filt_copy(i):
        return remote(filt_stage, filt.at[me], fsend.at[i], frecv.at[me], peer(i))

    def filt_arrival(i):
        return remote(filt_stage, filt.at[peer(i)], fsend.at[i], frecv.at[peer(i)], peer(i))

    @pl.when(has_right)
    def _():
        ph_copy().start()
        loop(0, QUADS, lambda q: g_copy(q).start())

    @pl.when(has_left)
    def _():
        loop(0, QUADS, lambda q: gm_copy(q).start())

    loop(1, SEQ, lambda i: filt_copy(i).start())
    filt[me] = filt_stage[...]

    def rest(c):
        for first, count in ((16, 48), (64, 64)):
            gated(c, first, count)
        for first in (128, 192):
            mixed(c, first, 64)

    loop(0, CHUNKS, rest)

    @pl.when(has_left)
    def _():
        ph_copy().wait_recv()

    @pl.when(jnp.logical_not(has_left))
    def _():
        ph[...] = jnp.zeros_like(ph)
        gx[0:LTAPS, :] = jnp.zeros((LTAPS, COLS), BF16)

    @pl.when(jnp.logical_not(has_right))
    def _():
        gmx[ROWS : ROWS + LTAPS, :] = jnp.zeros((LTAPS, COLS), BF16)
        gfh_recv[...] = jnp.zeros_like(gfh_recv)

    def edge(c):
        for s in range(3):
            xs[s, c, 0:EDGE, :] = ph[s, :, lanes(c)].astype(F32)
        mixed(c, 0, EDGE)
        gated(c, 0, EDGE)

    loop(0, CHUNKS, edge)

    @pl.when(has_left)
    def _():
        gm0_copy().start()

    loads[6].wait()
    loads[7].wait()

    def own_spectra(q):
        spec_g[:, wide(q)] = dot(fw[:, 0:ROWS], gx[LTAPS : LTAPS + ROWS, wide(q)])
        spec_gm[:, wide(q)] = dot(fw[:, 0:ROWS], gmx[0:ROWS, wide(q)])

    loop(0, QUADS, own_spectra)

    loop(1, SEQ, lambda i: filt_arrival(i).wait_recv())

    def unpack(d):
        for half in range(2):
            fperm[half, pl.ds(pl.multiple_of(d * 16, 16), 16), :] = filt[d, :, half * LANES : (half + 1) * LANES].astype(F32)

    loop(0, SEQ, unpack)
    for q in range(QUADS):
        parts = []
        for half in range(2):
            picked = [
                fperm[half, pl.ds(16 * first + OWN_TAPS * q + i, 8, stride=16), :]
                for i in range(OWN_TAPS)
                for first in range(0, SEQ, 8)
            ]
            parts.append(jnp.concatenate(picked, axis=0).astype(BF16))
        taps = jnp.concatenate(parts, axis=1)
        spec_h[:, WIDE * q : WIDE * (q + 1)] = dot(fw[:, ROWS + LTAPS :], taps) * (1.0 / HALF)

    @pl.when(has_right)
    def _():
        gm0_copy().wait_recv()

    def gf_copy(q):
        return remote(gfh_send.at[:, :, wide(q)], gfh_recv.at[:, :, wide(q)], gf_sem.at[0, q], gf_sem.at[1, q], left)

    def s_copy(p):
        return remote(gs_part.at[p], gs_recv.at[me], ssend.at[p], srecv.at[me], p)

    def s_arrival(i):
        return remote(gs_part.at[0], gs_recv.at[peer(i)], ssend.at[0], srecv.at[peer(i)], peer(i))

    def a_copy(i):
        return remote(gs_all.at[me], gs_all.at[me], asend.at[i], arecv.at[me], peer(i))

    def a_arrival(p):
        return remote(gs_all.at[p], gs_all.at[p], asend.at[0], arecv.at[p], p)

    def short_grad(c):
        for s in range(3):
            totals = [None] * STAPS
            for first in range(0, ROWS, 64):
                grad = fs[s, c, pl.ds(first, 64), :]
                for j in range(STAPS):
                    term = jnp.sum((grad * xs[s, c, pl.ds(EDGE + first - j, 64), :]).reshape(8, 8, LANES), axis=0)
                    totals[j] = term if totals[j] is None else totals[j] + term
            rows = [jnp.sum(t, axis=0, keepdims=True) for t in totals] + [jnp.zeros((1, LANES), F32)]
            gs_part[s * CHUNKS + c] = jnp.concatenate(rows, axis=0)

    def main(q):
        @pl.when(has_left)
        def _():
            g_copy(q).wait_recv()

        spec_g[:, wide(q)] += dot(fw[:, ROWS : ROWS + LTAPS], gx[0:LTAPS, wide(q)])

        @pl.when(has_right)
        def _():
            gm_copy(q).wait_recv()

        later = dot(fw[:, ROWS : ROWS + LTAPS], gmx[ROWS : ROWS + LTAPS, wide(q)])
        for first in range(0, HALF, 64):
            re, im = pl.ds(first, 64), pl.ds(HALF + first, 64)
            gc, gi = spec_g[re, wide(q)], spec_g[im, wide(q)]
            oc, oi = spec_gm[re, wide(q)], spec_gm[im, wide(q)]
            hc, hi = spec_h[re, wide(q)], spec_h[im, wide(q)]
            mc, mi = oc - later[first : first + 64], oi - later[HALF + first : HALF + first + 64]
            y1[re, :] = (gc * hc - gi * hi).astype(BF16)
            y1[im, :] = (gc * hi + gi * hc).astype(BF16)
            y2[re, :] = (mc * hc + mi * hi).astype(BF16)
            y2[im, :] = (mi * hc - mc * hi).astype(BF16)
            y3[re, wide(q)] = (oc * gc + oi * gi).astype(BF16)
            y3[im, wide(q)] = (oi * gc - oc * gi).astype(BF16)
        mixing = dot(iv[0:ROWS, :], y1[...])
        grad_gating = dot(iv[0:ROWS, :], y2[...])
        for half in range(2):
            c = 2 * q + half
            part = slice(half * LANES, (half + 1) * LANES)
            fs[0, c, 0:ROWS, :] = ov[:, lanes(c)].astype(F32) * mixing[:, part]
            fs[1, c, 0:ROWS, :] = grad_gating[:, part] * fkv[1, c]
            fs[2, c, 0:ROWS, :] = grad_gating[:, part] * fkv[0, c]
            for s in range(3):
                gfh_send[s, :, lanes(c)] = fs[s, c, 0:EDGE, :].astype(BF16)

        @pl.when(has_left)
        def _():
            gf_copy(q).start()

        for half in range(2):
            short_grad(2 * q + half)
            for s in range(3):
                piece = s * CHUNKS + 2 * q + half

                @pl.when(piece != me)
                def _():
                    s_copy(piece).start()

                @pl.when(piece == me)
                def _():
                    gs_recv[me] = gs_part[piece]

    loop(0, QUADS, main)

    def l_copy(i):
        return remote(gl_send.at[peer(i)], gl_recv.at[me], lsend.at[i], lrecv.at[me], peer(i))

    def l_arrival(i):
        return remote(gl_send.at[peer(i)], gl_recv.at[peer(i)], lsend.at[i], lrecv.at[peer(i)], peer(i))

    for q in range(QUADS):
        partial = dot(iv[ROWS:, :], y3[:, WIDE * q : WIDE * (q + 1)])
        for half in range(2):
            for i in range(OWN_TAPS):
                for first in range(0, SEQ, 8):
                    rows = partial[SEQ * i + first : SEQ * i + first + 8, half * LANES : (half + 1) * LANES]
                    lperm[half, pl.ds(16 * first + OWN_TAPS * q + i, 8, stride=16), :] = rows

    def pack(d):
        for half in range(2):
            gl_send[d, :, half * LANES : (half + 1) * LANES] = lperm[half, pl.ds(pl.multiple_of(d * 16, 16), 16), :].astype(BF16)

    loop(0, SEQ, pack)
    loop(1, SEQ, lambda i: l_copy(i).start())
    gl_recv[me] = gl_send[me]

    @pl.when(me < PIECES)
    def _():
        loop(1, SEQ, lambda i: s_arrival(i).wait_recv())
        total = gs_recv[0]
        for d in range(1, SEQ):
            total = total + gs_recv[d]
        gs_all[me] = total
        loop(1, SEQ, lambda i: a_copy(i).start())

    @pl.when(has_right)
    def _():
        loop(0, QUADS, lambda q: gf_copy(q).wait_recv())

    def gp_store(c):
        return pltpu.make_async_copy(gp_v.at[:, :, lanes(c)], gp_hbm.at[:, :, lanes(c)], store_sem.at[c])

    def back(c):
        for s in range(3):
            fs[s, c, ROWS : ROWS + EDGE, :] = gfh_recv[s, :, lanes(c)].astype(F32)
            for first in range(0, ROWS, 64):
                total = None
                for j in range(STAPS):
                    term = sfv[s, j : j + 1, lanes(c)] * fs[s, c, pl.ds(first + j, 64), :]
                    total = term if total is None else total + term
                gp_v[s, pl.ds(first, 64), lanes(c)] = total.astype(BF16)
        gp_store(c).start()

    loop(0, CHUNKS, back)

    loop(1, SEQ, lambda i: l_arrival(i).wait_recv())
    total = gl_recv[0].astype(F32)
    for d in range(1, SEQ):
        total = total + gl_recv[d].astype(F32)
    gl_sum[...] = total * (1.0 / HALF)
    for q in range(QUADS):
        gl_out[:, WIDE * q : WIDE * (q + 1)] = gl_sum[OWN_TAPS * q : OWN_TAPS * (q + 1), :]

    def a_wait(p):
        @pl.when(p != me)
        def _():
            a_arrival(p).wait_recv()

    loop(0, PIECES, a_wait)
    for s in range(3):
        for c in range(CHUNKS):
            gs_out[s, :, c * LANES : (c + 1) * LANES] = gs_all[s * CHUNKS + c, 0:STAPS, :]

    loop(0, CHUNKS, lambda c: gp_store(c).wait())

    @pl.when(has_right)
    def _():
        ph_copy().wait_send()
        loop(0, QUADS, lambda q: g_copy(q).wait_send())

    @pl.when(has_left)
    def _():
        loop(0, QUADS, lambda q: gm_copy(q).wait_send())
        gm0_copy().wait_send()
        loop(0, QUADS, lambda q: gf_copy(q).wait_send())

    loop(1, SEQ, lambda i: filt_copy(i).wait_send())
    loop(1, SEQ, lambda i: l_copy(i).wait_send())

    def s_sent(p):
        @pl.when(p != me)
        def _():
            s_copy(p).wait_send()

    loop(0, PIECES, s_sent)

    @pl.when(me < PIECES)
    def _():
        loop(1, SEQ, lambda i: a_copy(i).wait_send())


def on_device(projections, out_grad, short_filters, long_filter):
    forward, inverse = transforms()
    dma = pltpu.SemaphoreType.DMA
    vmem = pltpu.VMEM
    scratch = [
        vmem((3, ROWS, COLS), BF16),
        vmem((ROWS, COLS), BF16),
        vmem((3, STAPS, COLS), F32),
        vmem((OWN_TAPS, COLS), F32),
        vmem(forward.shape, BF16),
        vmem(inverse.shape, BF16),
        vmem((3, CHUNKS, EDGE + ROWS, LANES), F32),
        vmem((3, CHUNKS, ROWS + EDGE, LANES), F32),
        vmem((2, CHUNKS, ROWS, LANES), F32),
        vmem((LTAPS + ROWS, COLS), BF16),
        vmem((ROWS + LTAPS, COLS), BF16),
        vmem((3, EDGE, COLS), BF16),
        vmem((3, EDGE, COLS), BF16),
        vmem((3, EDGE, COLS), BF16),
        vmem((16, WIDE), BF16),
        vmem((SEQ, 16, WIDE), BF16),
        vmem((2, SEQ * 16, LANES), F32),
        vmem((POINTS, COLS), F32),
        vmem((POINTS, COLS), F32),
        vmem((POINTS, COLS), F32),
        vmem((POINTS, WIDE), BF16),
        vmem((POINTS, WIDE), BF16),
        vmem((POINTS, COLS), BF16),
        vmem((2, SEQ * 16, LANES), F32),
        vmem((SEQ, 16, WIDE), BF16),
        vmem((SEQ, 16, WIDE), BF16),
        vmem((16, WIDE), F32),
        vmem((PIECES, 8, LANES), F32),
        vmem((SEQ, 8, LANES), F32),
        vmem((PIECES, 8, LANES), F32),
        vmem((3, ROWS, COLS), BF16),
        dma((8,)), dma((CHUNKS,)), dma((2,)), dma((2, QUADS)), dma((2, QUADS)), dma((2,)), dma((2, QUADS)),
        dma((SEQ,)), dma((SEQ,)), dma((SEQ,)), dma((SEQ,)), dma((PIECES,)), dma((SEQ,)), dma((SEQ,)), dma((SEQ,)),
    ]
    hbm = pl.BlockSpec(memory_space=pl.ANY)
    in_vmem = pl.BlockSpec(memory_space=pltpu.VMEM)
    return pl.pallas_call(
        kernel,
        out_shape=(
            jax.ShapeDtypeStruct(projections.shape, BF16),
            jax.ShapeDtypeStruct(short_filters.shape, F32),
            jax.ShapeDtypeStruct(long_filter.shape, F32),
        ),
        in_specs=[hbm] * 6,
        out_specs=(hbm, in_vmem, in_vmem),
        scratch_shapes=scratch,
        compiler_params=pltpu.CompilerParams(collective_id=0, has_side_effects=True, vmem_limit_bytes=50 << 20),
    )(projections, out_grad, short_filters, long_filter, jnp.asarray(forward), jnp.asarray(inverse))


def solution(mesh):
    in_specs = (
        P(None, "seq", "tensor"),
        P("seq", "tensor"),
        P(None, None, "tensor"),
        P("seq", "tensor"),
    )
    out_specs = (P(None, "seq", "tensor"), P(None, None, "tensor"), P("seq", "tensor"))
    return jax.shard_map(on_device, mesh=mesh, in_specs=in_specs, out_specs=out_specs, check_vma=False)
```

time: 341 us -> 58.6 us (0.17)
  waiting for transfers between devices: 131 us -> 0 us
  local copies, waits for them, and re-layouts: 76.7 us -> 6.99 us
  blocking collectives: 52.2 us -> 0 us
  Pallas kernels: 0 us -> 50.7 us
  matrix products: 48.1 us -> 0 us
  between operations: 15.2 us -> 0.65 us
  starting transfers between devices: 9.41 us -> 0 us
  other arithmetic: 6.7 us -> 0 us
    psum x1 -> x0, waiting for transfers between devices: 128 us -> none  [on_device(): grad_short = lax.psum(partial_short, 'seq')]
    all_gather x1 -> x0, blocking collectives: 52.2 us -> none  [on_device(): full_taps = lax.all_gather(long_filter, 'seq', axis=0, tiled=True)]
    pallas_call x0 -> x1, Pallas kernels: none -> 50.7 us  [on_device(): pl.pallas_call(kernel, out_shape=(jax.ShapeDtypeStruct(projections.shape,...]
    conv_general_dilated x6 -> x0, matrix products: 48.1 us -> none  [correlate(): lax.conv_general_dilated(extended[None], taps[:, None, :], (1,), 'VALID',...]
    reshape x14 -> x0, local copies, waits for them, and re-layouts: 33.6 us -> none  [correlate(): lax.conv_general_dilated(extended[None], taps[:, None, :], (1,), 'VALID',...]
    conv_general_dilated x10 -> x0, local copies, waits for them, and re-layouts: 20.5 us -> none  [correlate(): lax.conv_general_dilated(extended[None], taps[:, None, :], (1,), 'VALID',...]
    ppermute x4 -> x0, starting transfers between devices: 9.37 us -> none  [passed_along(): return lax.ppermute(block, axis, route)]
    rev x4 -> x0, local copies, waits for them, and re-layouts: 6.48 us -> none  [the longest x1 2.91 us: on_device(): features = jax.vmap(correlate)(inputs_ext, short_filters[:, ::-1])]
  transfers between devices with their start and end apart: 5 -> 0, of which waited for: 2 -> 0; matrix products, arithmetic and copies ran while one was open for 20% -> 0% of each run, Pallas kernels for 0% -> 0%
where the time goes in v1:
time: 58.6 us; the launch traced here: 58.3 us
  Pallas kernels  50.7 us (87%)
  local copies, waits for them, and re-layouts  6.99 us (12%)
  between operations  0.65 us (1%)
    pallas_call x1, Pallas kernels, on_device(): pl.pallas_call(kernel, out_shape=(jax.ShapeDtypeStruct(projections.shape,...  50.7 us
    unnamed x13, local copies, waits for them, and re-layouts  6.99 us

profile of v1, /device:TPU:2, one launch (start us, length us, event | category | flops | bytes accessed | tf_op | source)
XLA Modules:
  0.0 58.3 jit_solution(16727090017679864164)
XLA Ops:
  0.6 0.0 copy-start
  0.6 1.0 %copy-done = bf16[256,1024]{1,0:T(8,128)(2,1)S(1)} copy-done((bf16[256,1024]{1,0:T(8,128)(2,1)S(1)}, bf16[256,1024]{1,0:T(8,128)(2,1)}, u32[]{:S(2)}) %copy-start) | copy-done | bytes 524312
  1.7 0.0 copy-start.1
  1.7 1.0 %copy-done.1 = bf16[384,512]{1,0:T(8,128)(2,1)S(1)} copy-done((bf16[384,512]{1,0:T(8,128)(2,1)S(1)}, bf16[384,512]{1,0:T(8,128)(2,1)}, u32[]{:S(2)}) %copy-start.1) | copy-done | bytes 393240
  2.7 0.0 copy-start.2
  2.7 1.0 %copy-done.2 = bf16[384,384]{1,0:T(8,128)(2,1)S(1)} copy-done((bf16[384,384]{1,0:T(8,128)(2,1)S(1)}, bf16[384,384]{1,0:T(8,128)(2,1)}, u32[]{:S(2)}) %copy-start.2) | copy-done | bytes 294936
  3.6 0.0 copy-start.3
  3.6 0.9 %copy-done.3 = f32[3,7,1024]{2,1,0:T(8,128)S(1)} copy-done((f32[3,7,1024]{2,1,0:T(8,128)S(1)}, f32[3,7,1024]{2,1,0:T(8,128)}, u32[]{:S(2)}) %copy-start.3) | copy-done | bytes 86040
  4.5 0.0 copy-start.4
  4.5 0.7 %copy-done.4 = f32[4,1024]{1,0:T(4,128)S(1)} copy-done((f32[4,1024]{1,0:T(4,128)S(1)}, f32[4,1024]{1,0:T(4,128)}, u32[]{:S(2)}) %copy-start.4) | copy-done | bytes 16408
  5.2 50.7 %shard_map.85 = (bf16[3,256,1024]{2,1,0:T(8,128)(2,1)S(1)}, f32[3,7,1024]{2,1,0:T(8,128)S(1)}, f32[4,1024]{1,0:T(4,128)S(1)}) custom-call(bf16[3,256,1024]{2,1,0:T(8,128)(2,1)} %proj_hbm.1, bf16[256,1024]{1,0:T(8,128)(2,1)S(1)} %copy-done, f32[3,7,1024]{2,1,0:T(8,128)S(1)} %copy-done.3, f32[4,1024]{1,0:T(4,128)S(1)} %copy-done.4, ...), custom_call_target="tpu_custom_call" | custom-call | tf_op jit(solution)/shard_map/pallas_call | solution.py:464
  55.9 1.1 %copy.12 = bf16[3,256,1024]{2,1,0:T(8,128)(2,1)} copy(bf16[3,256,1024]{2,1,0:T(8,128)(2,1)S(1)} %get-tuple-element.6) | data formatting | bytes 3145728
  57.1 0.6 %copy.13 = f32[3,7,1024]{2,1,0:T(8,128)} copy(f32[3,7,1024]{2,1,0:T(8,128)S(1)} %get-tuple-element.7) | data formatting | bytes 172032
  57.7 0.6 %copy.14 = f32[4,1024]{1,0:T(4,128)} copy(f32[4,1024]{1,0:T(4,128)S(1)} %get-tuple-element.8) | data formatting | bytes 32768
Async XLA Ops:
  0.6 1.0 %copy-start = (bf16[256,1024]{1,0:T(8,128)(2,1)S(1)}, bf16[256,1024]{1,0:T(8,128)(2,1)}, u32[]{:S(2)}) copy-start(bf16[256,1024]{1,0:T(8,128)(2,1)} %og_hbm.1) | copy-start | bytes 1572868
  1.7 1.0 %copy-start.1 = (bf16[384,512]{1,0:T(8,128)(2,1)S(1)}, bf16[384,512]{1,0:T(8,128)(2,1)}, u32[]{:S(2)}) copy-start(bf16[384,512]{1,0:T(8,128)(2,1)} %constant.4.clone.fw_hbm) | copy-start | bytes 1179652
  2.7 1.0 %copy-start.2 = (bf16[384,384]{1,0:T(8,128)(2,1)S(1)}, bf16[384,384]{1,0:T(8,128)(2,1)}, u32[]{:S(2)}) copy-start(bf16[384,384]{1,0:T(8,128)(2,1)} %constant.5.clone.iv_hbm) | copy-start | bytes 884740
  3.6 0.9 %copy-start.3 = (f32[3,7,1024]{2,1,0:T(8,128)S(1)}, f32[3,7,1024]{2,1,0:T(8,128)}, u32[]{:S(2)}) copy-start(f32[3,7,1024]{2,1,0:T(8,128)} %sf_hbm.1) | copy-start | bytes 258052
  4.5 0.7 %copy-start.4 = (f32[4,1024]{1,0:T(4,128)S(1)}, f32[4,1024]{1,0:T(4,128)}, u32[]{:S(2)}) copy-start(f32[4,1024]{1,0:T(4,128)} %lf_hbm.1) | copy-start | bytes 49156

commit v2 on v1

--- a/solution.py
+++ b/solution.py
@@ -25,6 +25,10 @@
 HALF = POINTS // 2
 EDGE = 16
 PIECES = 3 * CHUNKS
+ROW = 4
+COLUMN = 8
+FIRST_OWNER = 12
+HALO = STAPS - 1
 
 
 def transforms():
@@ -59,8 +63,8 @@
     proj_hbm, og_hbm, sf_hbm, lf_hbm, fw_hbm, iv_hbm,
     gp_hbm, gs_out, gl_out,
     pv, ov, sfv, lfv, fw, iv,
-    xs, fs, fkv, gx, gmx, ph, gfh_send, gfh_recv,
-    filt_stage, filt, fperm, spec_g, spec_gm, spec_h, y1, y2, y3,
+    xs, fs, fkv, gx, gmx, ph_stage, ph_send, ph_recv, gf_stage, gf_send, gf_recv,
+    filt_a, filt_b, fperm, spec_g, spec_gm, spec_h, y1, y2,
     lperm, gl_send, gl_recv, gl_sum, gs_part, gs_recv, gs_all, gp_v,
     load_sem, store_sem, ph_sem, g_sem, gm_sem, gm0_sem, gf_sem,
     fsend, frecv, lsend, lrecv, ssend, srecv, asend, arecv,
@@ -81,8 +85,18 @@
     def loop(low, high, body):
         lax.fori_loop(low, high, lambda i, _: (body(i), 0)[1], 0)
 
+    y, z = lax.rem(me, ROW), lax.div(me, ROW)
+
+    def in_row(i):
+        return z * ROW + lax.rem(y + i, ROW)
+
+    def in_column(i):
+        return lax.rem(z + i, COLUMN) * ROW + y
+
     barrier = pltpu.get_barrier_semaphore()
-    loop(1, SEQ, lambda i: pl.semaphore_signal(barrier, inc=1, device_id={"seq": peer(i)}, device_id_type=MESH))
+    greeted = [left, right] + [in_row(i) for i in range(1, ROW)] + [in_column(i) for i in range(1, COLUMN)]
+    for other in greeted:
+        pl.semaphore_signal(barrier, inc=1, device_id={"seq": other}, device_id_type=MESH)
 
     loads = [
         pltpu.make_async_copy(src, dst, load_sem.at[n])
@@ -139,13 +153,33 @@
     for q in range(QUADS):
         lperm[0, OWN_TAPS * q : OWN_TAPS * (q + 1), :] = lfv[:, WIDE * q : WIDE * q + LANES]
         lperm[1, OWN_TAPS * q : OWN_TAPS * (q + 1), :] = lfv[:, WIDE * q + LANES : WIDE * (q + 1)]
-    filt_stage[:, 0:LANES] = lperm[0, 0:16, :].astype(BF16)
-    filt_stage[:, LANES:WIDE] = lperm[1, 0:16, :].astype(BF16)
-
-    pl.semaphore_wait(barrier, SEQ - 1)
+    filt_a[z, y] = lperm[0, 0:16, :].astype(BF16)
+    filt_b[y, z] = lperm[1, 0:16, :].astype(BF16)
+
+    def fold(stage, source, first, packed):
+        for c in range(CHUNKS):
+            stage[c, 0:6, :] = source[0, c, first : first + 6, :]
+            stage[c, 6:12, :] = source[1, c, first : first + 6, :]
+            stage[c, 12:16, :] = source[2, c, first : first + 4, :]
+            stage[CHUNKS, 2 * c : 2 * c + 2, :] = source[2, c, first + 4 : first + 6, :]
+        for c in range(CHUNKS + 1):
+            packed[:, LANES * c : LANES * (c + 1)] = stage[c].astype(BF16)
+
+    def unfold(packed, stage, target, first):
+        for c in range(CHUNKS + 1):
+            stage[c] = packed[:, LANES * c : LANES * (c + 1)].astype(F32)
+        for c in range(CHUNKS):
+            target[0, c, first : first + 6, :] = stage[c, 0:6, :]
+            target[1, c, first : first + 6, :] = stage[c, 6:12, :]
+            target[2, c, first : first + 4, :] = stage[c, 12:16, :]
+            target[2, c, first + 4 : first + 6, :] = stage[CHUNKS, 2 * c : 2 * c + 2, :]
+
+    fold(ph_stage, xs, EDGE + ROWS - HALO, ph_send)
+
+    pl.semaphore_wait(barrier, len(greeted))
 
     def ph_copy():
-        return remote(pv.at[:, pl.ds(ROWS - EDGE, EDGE), :], ph, ph_sem.at[0], ph_sem.at[1], right)
+        return remote(ph_send, ph_recv, ph_sem.at[0], ph_sem.at[1], right)
 
     def g_copy(q):
         return remote(gx.at[pl.ds(ROWS, LTAPS), wide(q)], gx.at[pl.ds(0, LTAPS), wide(q)], g_sem.at[0, q], g_sem.at[1, q], right)
@@ -159,11 +193,20 @@
     def gm0_copy():
         return remote(gmx.at[pl.ds(0, EDGE), :], gmx.at[pl.ds(ROWS, EDGE), :], gm0_sem.at[0], gm0_sem.at[1], left)
 
-    def filt_copy(i):
-        return remote(filt_stage, filt.at[me], fsend.at[i], frecv.at[me], peer(i))
-
-    def filt_arrival(i):
-        return remote(filt_stage, filt.at[peer(i)], fsend.at[i], frecv.at[peer(i)], peer(i))
+    def a1_copy(i):
+        return remote(filt_a.at[z, y], filt_a.at[z, y], fsend.at[i], frecv.at[i], in_row(i))
+
+    def a2_copy(i):
+        return remote(filt_a.at[z], filt_a.at[z], fsend.at[ROW + i], frecv.at[ROW + i], in_column(i))
+
+    def b1_copy(i):
+        return remote(filt_b.at[y, z], filt_b.at[y, z], fsend.at[12 + i], frecv.at[12 + i], in_column(i))
+
+    def b2_copy(i):
+        return remote(filt_b.at[y], filt_b.at[y], fsend.at[20 + i], frecv.at[20 + i], in_row(i))
+
+    loop(1, ROW, lambda i: a1_copy(i).start())
+    loop(1, COLUMN, lambda i: b1_copy(i).start())
 
     @pl.when(has_right)
     def _():
@@ -173,9 +216,6 @@
     @pl.when(has_left)
     def _():
         loop(0, QUADS, lambda q: gm_copy(q).start())
-
-    loop(1, SEQ, lambda i: filt_copy(i).start())
-    filt[me] = filt_stage[...]
 
     def rest(c):
         for first, count in ((16, 48), (64, 64)):
@@ -191,17 +231,17 @@
 
     @pl.when(jnp.logical_not(has_left))
     def _():
-        ph[...] = jnp.zeros_like(ph)
+        ph_recv[...] = jnp.zeros_like(ph_recv)
         gx[0:LTAPS, :] = jnp.zeros((LTAPS, COLS), BF16)
 
     @pl.when(jnp.logical_not(has_right))
     def _():
         gmx[ROWS : ROWS + LTAPS, :] = jnp.zeros((LTAPS, COLS), BF16)
-        gfh_recv[...] = jnp.zeros_like(gfh_recv)
+        gf_recv[...] = jnp.zeros_like(gf_recv)
+
+    unfold(ph_recv, ph_stage, xs, EDGE - HALO)
 
     def edge(c):
-        for s in range(3):
-            xs[s, c, 0:EDGE, :] = ph[s, :, lanes(c)].astype(F32)
         mixed(c, 0, EDGE)
         gated(c, 0, EDGE)
 
@@ -210,6 +250,9 @@
     @pl.when(has_left)
     def _():
         gm0_copy().start()
+
+    loop(1, ROW, lambda i: a1_copy(i).wait_recv())
+    loop(1, COLUMN, lambda i: a2_copy(i).start())
 
     loads[6].wait()
     loads[7].wait()
@@ -220,11 +263,53 @@
 
     loop(0, QUADS, own_spectra)
 
-    loop(1, SEQ, lambda i: filt_arrival(i).wait_recv())
+    loop(1, COLUMN, lambda i: b1_copy(i).wait_recv())
+    loop(1, ROW, lambda i: b2_copy(i).start())
+
+    for q in range(QUADS):
+
+        @pl.when(has_left)
+        def _():
+            g_copy(q).wait_recv()
+
+        spec_g[:, WIDE * q : WIDE * (q + 1)] += dot(fw[:, ROWS : ROWS + LTAPS], gx[0:LTAPS, WIDE * q : WIDE * (q + 1)])
+        for first in range(0, HALF, 64):
+            re, im = pl.ds(first, 64), pl.ds(HALF + first, 64)
+            cols = pl.ds(WIDE * q, WIDE)
+            gc, gi = spec_g[re, cols], spec_g[im, cols]
+            oc, oi = spec_gm[re, cols], spec_gm[im, cols]
+            y1[re, :] = (oc * gc + oi * gi).astype(BF16)
+            y1[im, :] = (oi * gc - oc * gi).astype(BF16)
+        partial = dot(iv[ROWS:, :], y1[...])
+        for half in range(2):
+            for i in range(OWN_TAPS):
+                for first in range(0, SEQ, 8):
+                    rows = partial[SEQ * i + first : SEQ * i + first + 8, half * LANES : (half + 1) * LANES]
+                    lperm[half, pl.ds(16 * first + OWN_TAPS * q + i, 8, stride=16), :] = rows
+
+    def pack(d):
+        for half in range(2):
+            gl_send[d, :, half * LANES : (half + 1) * LANES] = lperm[half, pl.ds(pl.multiple_of(d * 16, 16), 16), :].astype(BF16)
+
+    loop(0, SEQ, pack)
+
+    loop(1, COLUMN, lambda i: a2_copy(i).wait_recv())
+    loop(1, ROW, lambda i: b2_copy(i).wait_recv())
+
+    def l_copy(i):
+        return remote(gl_send.at[peer(i)], gl_recv.at[me], lsend.at[i], lrecv.at[me], peer(i))
+
+    def l_arrival(i):
+        return remote(gl_send.at[peer(i)], gl_recv.at[peer(i)], lsend.at[i], lrecv.at[peer(i)], peer(i))
+
+    loop(1, SEQ, lambda i: l_copy(i).start())
+    gl_recv[me] = gl_send[me]
 
     def unpack(d):
-        for half in range(2):
-            fperm[half, pl.ds(pl.multiple_of(d * 16, 16), 16), :] = filt[d, :, half * LANES : (half + 1) * LANES].astype(F32)
+        rows = pl.ds(pl.multiple_of(d * 16, 16), 16)
+        dz, dy = lax.div(d, ROW), lax.rem(d, ROW)
+        fperm[0, rows, :] = filt_a[dz, dy].astype(F32)
+        fperm[1, rows, :] = filt_b[dy, dz].astype(F32)
 
     loop(0, SEQ, unpack)
     for q in range(QUADS):
@@ -243,20 +328,25 @@
     def _():
         gm0_copy().wait_recv()
 
-    def gf_copy(q):
-        return remote(gfh_send.at[:, :, wide(q)], gfh_recv.at[:, :, wide(q)], gf_sem.at[0, q], gf_sem.at[1, q], left)
+    def gf_copy():
+        return remote(gf_send, gf_recv, gf_sem.at[0], gf_sem.at[1], left)
+
+    my_piece = lax.rem(me + SEQ - FIRST_OWNER, SEQ)
+
+    def owner(p):
+        return lax.rem(p + FIRST_OWNER, SEQ)
 
     def s_copy(p):
-        return remote(gs_part.at[p], gs_recv.at[me], ssend.at[p], srecv.at[me], p)
+        return remote(gs_part.at[p], gs_recv.at[me], ssend.at[p], srecv.at[me], owner(p))
 
     def s_arrival(i):
         return remote(gs_part.at[0], gs_recv.at[peer(i)], ssend.at[0], srecv.at[peer(i)], peer(i))
 
-    def a_copy(i):
-        return remote(gs_all.at[me], gs_all.at[me], asend.at[i], arecv.at[me], peer(i))
+    def a_copy(d):
+        return remote(gs_all.at[my_piece], gs_all.at[my_piece], asend.at[d], arecv.at[my_piece], d)
 
     def a_arrival(p):
-        return remote(gs_all.at[p], gs_all.at[p], asend.at[0], arecv.at[p], p)
+        return remote(gs_all.at[p], gs_all.at[p], asend.at[0], arecv.at[p], owner(p))
 
     def short_grad(c):
         for s in range(3):
@@ -267,15 +357,9 @@
                     term = jnp.sum((grad * xs[s, c, pl.ds(EDGE + first - j, 64), :]).reshape(8, 8, LANES), axis=0)
                     totals[j] = term if totals[j] is None else totals[j] + term
             rows = [jnp.sum(t, axis=0, keepdims=True) for t in totals] + [jnp.zeros((1, LANES), F32)]
-            gs_part[s * CHUNKS + c] = jnp.concatenate(rows, axis=0)
+            gs_part[3 * c + s] = jnp.concatenate(rows, axis=0)
 
     def main(q):
-        @pl.when(has_left)
-        def _():
-            g_copy(q).wait_recv()
-
-        spec_g[:, wide(q)] += dot(fw[:, ROWS : ROWS + LTAPS], gx[0:LTAPS, wide(q)])
-
         @pl.when(has_right)
         def _():
             gm_copy(q).wait_recv()
@@ -291,8 +375,6 @@
             y1[im, :] = (gc * hi + gi * hc).astype(BF16)
             y2[re, :] = (mc * hc + mi * hi).astype(BF16)
             y2[im, :] = (mi * hc - mc * hi).astype(BF16)
-            y3[re, wide(q)] = (oc * gc + oi * gi).astype(BF16)
-            y3[im, wide(q)] = (oi * gc - oc * gi).astype(BF16)
         mixing = dot(iv[0:ROWS, :], y1[...])
         grad_gating = dot(iv[0:ROWS, :], y2[...])
         for half in range(2):
@@ -301,78 +383,70 @@
             fs[0, c, 0:ROWS, :] = ov[:, lanes(c)].astype(F32) * mixing[:, part]
             fs[1, c, 0:ROWS, :] = grad_gating[:, part] * fkv[1, c]
             fs[2, c, 0:ROWS, :] = grad_gating[:, part] * fkv[0, c]
-            for s in range(3):
-                gfh_send[s, :, lanes(c)] = fs[s, c, 0:EDGE, :].astype(BF16)
-
-        @pl.when(has_left)
-        def _():
-            gf_copy(q).start()
 
         for half in range(2):
             short_grad(2 * q + half)
             for s in range(3):
-                piece = s * CHUNKS + 2 * q + half
-
-                @pl.when(piece != me)
+                piece = 3 * (2 * q + half) + s
+
+                @pl.when(piece != my_piece)
                 def _():
                     s_copy(piece).start()
 
-                @pl.when(piece == me)
+                @pl.when(piece == my_piece)
                 def _():
                     gs_recv[me] = gs_part[piece]
 
     loop(0, QUADS, main)
 
-    def l_copy(i):
-        return remote(gl_send.at[peer(i)], gl_recv.at[me], lsend.at[i], lrecv.at[me], peer(i))
-
-    def l_arrival(i):
-        return remote(gl_send.at[peer(i)], gl_recv.at[peer(i)], lsend.at[i], lrecv.at[peer(i)], peer(i))
-
-    for q in range(QUADS):
-        partial = dot(iv[ROWS:, :], y3[:, WIDE * q : WIDE * (q + 1)])
-        for half in range(2):
-            for i in range(OWN_TAPS):
-                for first in range(0, SEQ, 8):
-                    rows = partial[SEQ * i + first : SEQ * i + first + 8, half * LANES : (half + 1) * LANES]
-                    lperm[half, pl.ds(16 * first + OWN_TAPS * q + i, 8, stride=16), :] = rows
-
-    def pack(d):
-        for half in range(2):
-            gl_send[d, :, half * LANES : (half + 1) * LANES] = lperm[half, pl.ds(pl.multiple_of(d * 16, 16), 16), :].astype(BF16)
-
-    loop(0, SEQ, pack)
-    loop(1, SEQ, lambda i: l_copy(i).start())
-    gl_recv[me] = gl_send[me]
-
-    @pl.when(me < PIECES)
+    fold(gf_stage, fs, 0, gf_send)
+
+    @pl.when(has_left)
+    def _():
+        gf_copy().start()
+
+    def back(c, first, count):
+        for s in range(3):
+            total = None
+            for j in range(STAPS):
+                term = sfv[s, j : j + 1, lanes(c)] * fs[s, c, pl.ds(first + j, count), :]
+                total = term if total is None else total + term
+            gp_v[s, pl.ds(first, count), lanes(c)] = total.astype(BF16)
+
+    def back_bulk(c):
+        for first, count in ((0, 64), (64, 64), (128, 64), (192, 48)):
+            back(c, first, count)
+
+    loop(0, CHUNKS, back_bulk)
+
+    def gp_store(c):
+        return pltpu.make_async_copy(gp_v.at[:, :, lanes(c)], gp_hbm.at[:, :, lanes(c)], store_sem.at[c])
+
+    @pl.when(has_right)
+    def _():
+        gf_copy().wait_recv()
+
+    unfold(gf_recv, gf_stage, fs, ROWS)
+
+    def back_edge(c):
+        back(c, ROWS - EDGE, EDGE)
+        gp_store(c).start()
+
+    loop(0, CHUNKS, back_edge)
+
+    def hand_out(d):
+        @pl.when(d != me)
+        def _():
+            a_copy(d).start()
+
+    @pl.when(my_piece < PIECES)
     def _():
         loop(1, SEQ, lambda i: s_arrival(i).wait_recv())
         total = gs_recv[0]
         for d in range(1, SEQ):
             total = total + gs_recv[d]
-        gs_all[me] = total
-        loop(1, SEQ, lambda i: a_copy(i).start())
-
-    @pl.when(has_right)
-    def _():
-        loop(0, QUADS, lambda q: gf_copy(q).wait_recv())
-
-    def gp_store(c):
-        return pltpu.make_async_copy(gp_v.at[:, :, lanes(c)], gp_hbm.at[:, :, lanes(c)], store_sem.at[c])
-
-    def back(c):
-        for s in range(3):
-            fs[s, c, ROWS : ROWS + EDGE, :] = gfh_recv[s, :, lanes(c)].astype(F32)
-            for first in range(0, ROWS, 64):
-                total = None
-                for j in range(STAPS):
-                    term = sfv[s, j : j + 1, lanes(c)] * fs[s, c, pl.ds(first + j, 64), :]
-                    total = term if total is None else total + term
-                gp_v[s, pl.ds(first, 64), lanes(c)] = total.astype(BF16)
-        gp_store(c).start()
-
-    loop(0, CHUNKS, back)
+        gs_all[my_piece] = total
+        loop(0, SEQ, hand_out)
 
     loop(1, SEQ, lambda i: l_arrival(i).wait_recv())
     total = gl_recv[0].astype(F32)
@@ -382,42 +456,52 @@
     for q in range(QUADS):
         gl_out[:, WIDE * q : WIDE * (q + 1)] = gl_sum[OWN_TAPS * q : OWN_TAPS * (q + 1), :]
 
+    @pl.when(has_right)
+    def _():
+        ph_copy().wait_send()
+        loop(0, QUADS, lambda q: g_copy(q).wait_send())
+
+    @pl.when(has_left)
+    def _():
+        loop(0, QUADS, lambda q: gm_copy(q).wait_send())
+        gm0_copy().wait_send()
+        gf_copy().wait_send()
+
+    for i in range(1, ROW):
+        a1_copy(i).wait_send()
+        b2_copy(i).wait_send()
+    for i in range(1, COLUMN):
+        a2_copy(i).wait_send()
+        b1_copy(i).wait_send()
+    loop(1, SEQ, lambda i: l_copy(i).wait_send())
+
+    def s_sent(p):
+        @pl.when(p != my_piece)
+        def _():
+            s_copy(p).wait_send()
+
+    loop(0, PIECES, s_sent)
+
+    def a_sent(d):
+        @pl.when(d != me)
+        def _():
+            a_copy(d).wait_send()
+
+    @pl.when(my_piece < PIECES)
+    def _():
+        loop(0, SEQ, a_sent)
+
+    loop(0, CHUNKS, lambda c: gp_store(c).wait())
+
     def a_wait(p):
-        @pl.when(p != me)
+        @pl.when(p != my_piece)
         def _():
             a_arrival(p).wait_recv()
 
     loop(0, PIECES, a_wait)
     for s in range(3):
         for c in range(CHUNKS):
-            gs_out[s, :, c * LANES : (c + 1) * LANES] = gs_all[s * CHUNKS + c, 0:STAPS, :]
-
-    loop(0, CHUNKS, lambda c: gp_store(c).wait())
-
-    @pl.when(has_right)
-    def _():
-        ph_copy().wait_send()
-        loop(0, QUADS, lambda q: g_copy(q).wait_send())
-
-    @pl.when(has_left)
-    def _():
-        loop(0, QUADS, lambda q: gm_copy(q).wait_send())
-        gm0_copy().wait_send()
-        loop(0, QUADS, lambda q: gf_copy(q).wait_send())
-
-    loop(1, SEQ, lambda i: filt_copy(i).wait_send())
-    loop(1, SEQ, lambda i: l_copy(i).wait_send())
-
-    def s_sent(p):
-        @pl.when(p != me)
-        def _():
-            s_copy(p).wait_send()
-
-    loop(0, PIECES, s_sent)
-
-    @pl.when(me < PIECES)
-    def _():
-        loop(1, SEQ, lambda i: a_copy(i).wait_send())
+            gs_out[s, :, c * LANES : (c + 1) * LANES] = gs_all[3 * c + s, 0:STAPS, :]
 
 
 def on_device(projections, out_grad, short_filters, long_filter):
@@ -436,18 +520,20 @@
         vmem((2, CHUNKS, ROWS, LANES), F32),
         vmem((LTAPS + ROWS, COLS), BF16),
         vmem((ROWS + LTAPS, COLS), BF16),
-        vmem((3, EDGE, COLS), BF16),
-        vmem((3, EDGE, COLS), BF16),
-        vmem((3, EDGE, COLS), BF16),
-        vmem((16, WIDE), BF16),
-        vmem((SEQ, 16, WIDE), BF16),
+        vmem((CHUNKS + 1, EDGE, LANES), F32),
+        vmem((EDGE, COLS + LANES), BF16),
+        vmem((EDGE, COLS + LANES), BF16),
+        vmem((CHUNKS + 1, EDGE, LANES), F32),
+        vmem((EDGE, COLS + LANES), BF16),
+        vmem((EDGE, COLS + LANES), BF16),
+        vmem((COLUMN, ROW, 16, LANES), BF16),
+        vmem((ROW, COLUMN, 16, LANES), BF16),
         vmem((2, SEQ * 16, LANES), F32),
         vmem((POINTS, COLS), F32),
         vmem((POINTS, COLS), F32),
         vmem((POINTS, COLS), F32),
         vmem((POINTS, WIDE), BF16),
         vmem((POINTS, WIDE), BF16),
-        vmem((POINTS, COLS), BF16),
         vmem((2, SEQ * 16, LANES), F32),
         vmem((SEQ, 16, WIDE), BF16),
         vmem((SEQ, 16, WIDE), BF16),
@@ -456,10 +542,10 @@
         vmem((SEQ, 8, LANES), F32),
         vmem((PIECES, 8, LANES), F32),
         vmem((3, ROWS, COLS), BF16),
-        dma((8,)), dma((CHUNKS,)), dma((2,)), dma((2, QUADS)), dma((2, QUADS)), dma((2,)), dma((2, QUADS)),
+        dma((8,)), dma((CHUNKS,)), dma((2,)), dma((2, QUADS)), dma((2, QUADS)), dma((2,)), dma((2,)),
         dma((SEQ,)), dma((SEQ,)), dma((SEQ,)), dma((SEQ,)), dma((PIECES,)), dma((SEQ,)), dma((SEQ,)), dma((SEQ,)),
     ]
-    hbm = pl.BlockSpec(memory_space=pl.ANY)
+    hbm = pl.BlockSpec(memory_space=pltpu.HBM)
     in_vmem = pl.BlockSpec(memory_space=pltpu.VMEM)
     return pl.pallas_call(
         kernel,

time: 58.6 us -> 48.5 us (0.83)
  Pallas kernels: 50.7 us -> 40.5 us
    pallas_call x1, Pallas kernels: 50.7 us -> 40.5 us  [on_device(): pl.pallas_call(kernel, out_shape=(jax.ShapeDtypeStruct(projections.shape,...]
where the time goes in v2:
time: 48.5 us; the launch traced here: 48.2 us
  Pallas kernels  40.5 us (84%)
  local copies, waits for them, and re-layouts  6.99 us (14%)
  between operations  0.65 us (1%)
    pallas_call x1, Pallas kernels, on_device(): pl.pallas_call(kernel, out_shape=(jax.ShapeDtypeStruct(projections.shape,...  40.5 us
    unnamed x13, local copies, waits for them, and re-layouts  6.99 us

profile of v2, /device:TPU:2, one launch (start us, length us, event | category | flops | bytes accessed | tf_op | source)
XLA Modules:
  0.0 48.2 jit_solution(11686300165842763501)
XLA Ops:
  0.6 0.0 copy-start
  0.6 1.0 %copy-done = bf16[256,1024]{1,0:T(8,128)(2,1)S(1)} copy-done((bf16[256,1024]{1,0:T(8,128)(2,1)S(1)}, bf16[256,1024]{1,0:T(8,128)(2,1)}, u32[]{:S(2)}) %copy-start) | copy-done | bytes 524312
  1.7 0.0 copy-start.1
  1.7 1.0 %copy-done.1 = bf16[384,512]{1,0:T(8,128)(2,1)S(1)} copy-done((bf16[384,512]{1,0:T(8,128)(2,1)S(1)}, bf16[384,512]{1,0:T(8,128)(2,1)}, u32[]{:S(2)}) %copy-start.1) | copy-done | bytes 393240
  2.7 0.0 copy-start.2
  2.7 1.0 %copy-done.2 = bf16[384,384]{1,0:T(8,128)(2,1)S(1)} copy-done((bf16[384,384]{1,0:T(8,128)(2,1)S(1)}, bf16[384,384]{1,0:T(8,128)(2,1)}, u32[]{:S(2)}) %copy-start.2) | copy-done | bytes 294936
  3.6 0.0 copy-start.3
  3.6 0.9 %copy-done.3 = f32[3,7,1024]{2,1,0:T(8,128)S(1)} copy-done((f32[3,7,1024]{2,1,0:T(8,128)S(1)}, f32[3,7,1024]{2,1,0:T(8,128)}, u32[]{:S(2)}) %copy-start.3) | copy-done | bytes 86040
  4.5 0.0 copy-start.4
  4.5 0.7 %copy-done.4 = f32[4,1024]{1,0:T(4,128)S(1)} copy-done((f32[4,1024]{1,0:T(4,128)S(1)}, f32[4,1024]{1,0:T(4,128)}, u32[]{:S(2)}) %copy-start.4) | copy-done | bytes 16408
  5.2 40.5 %shard_map.85 = (bf16[3,256,1024]{2,1,0:T(8,128)(2,1)S(1)}, f32[3,7,1024]{2,1,0:T(8,128)S(1)}, f32[4,1024]{1,0:T(4,128)S(1)}) custom-call(bf16[3,256,1024]{2,1,0:T(8,128)(2,1)} %proj_hbm.1, bf16[256,1024]{1,0:T(8,128)(2,1)S(1)} %copy-done, f32[3,7,1024]{2,1,0:T(8,128)S(1)} %copy-done.3, f32[4,1024]{1,0:T(4,128)S(1)} %copy-done.4, ...), custom_call_target="tpu_custom_call" | custom-call | tf_op jit(solution)/shard_map/pallas_call | solution.py:550
  45.8 1.1 %copy.12 = bf16[3,256,1024]{2,1,0:T(8,128)(2,1)} copy(bf16[3,256,1024]{2,1,0:T(8,128)(2,1)S(1)} %get-tuple-element.6) | data formatting | bytes 3145728
  46.9 0.6 %copy.13 = f32[3,7,1024]{2,1,0:T(8,128)} copy(f32[3,7,1024]{2,1,0:T(8,128)S(1)} %get-tuple-element.7) | data formatting | bytes 172032
  47.6 0.6 %copy.14 = f32[4,1024]{1,0:T(4,128)} copy(f32[4,1024]{1,0:T(4,128)S(1)} %get-tuple-element.8) | data formatting | bytes 32768
Async XLA Ops:
  0.6 1.0 %copy-start = (bf16[256,1024]{1,0:T(8,128)(2,1)S(1)}, bf16[256,1024]{1,0:T(8,128)(2,1)}, u32[]{:S(2)}) copy-start(bf16[256,1024]{1,0:T(8,128)(2,1)} %og_hbm.1) | copy-start | bytes 1572868
  1.7 1.0 %copy-start.1 = (bf16[384,512]{1,0:T(8,128)(2,1)S(1)}, bf16[384,512]{1,0:T(8,128)(2,1)}, u32[]{:S(2)}) copy-start(bf16[384,512]{1,0:T(8,128)(2,1)} %constant.4.clone.fw_hbm) | copy-start | bytes 1179652
  2.7 1.0 %copy-start.2 = (bf16[384,384]{1,0:T(8,128)(2,1)S(1)}, bf16[384,384]{1,0:T(8,128)(2,1)}, u32[]{:S(2)}) copy-start(bf16[384,384]{1,0:T(8,128)(2,1)} %constant.5.clone.iv_hbm) | copy-start | bytes 884740
  3.6 0.9 %copy-start.3 = (f32[3,7,1024]{2,1,0:T(8,128)S(1)}, f32[3,7,1024]{2,1,0:T(8,128)}, u32[]{:S(2)}) copy-start(f32[3,7,1024]{2,1,0:T(8,128)} %sf_hbm.1) | copy-start | bytes 258052
  4.5 0.7 %copy-start.4 = (f32[4,1024]{1,0:T(4,128)S(1)}, f32[4,1024]{1,0:T(4,128)}, u32[]{:S(2)}) copy-start(f32[4,1024]{1,0:T(4,128)} %lf_hbm.1) | copy-start | bytes 49156

commit v3 on v2

--- a/solution.py
+++ b/solution.py
@@ -61,12 +61,12 @@
 
 def kernel(
     proj_hbm, og_hbm, sf_hbm, lf_hbm, fw_hbm, iv_hbm,
-    gp_hbm, gs_out, gl_out,
+    gp_v, gs_out, gl_out,
     pv, ov, sfv, lfv, fw, iv,
     xs, fs, fkv, gx, gmx, ph_stage, ph_send, ph_recv, gf_stage, gf_send, gf_recv,
     filt_a, filt_b, fperm, spec_g, spec_gm, spec_h, y1, y2,
-    lperm, gl_send, gl_recv, gl_sum, gs_part, gs_recv, gs_all, gp_v,
-    load_sem, store_sem, ph_sem, g_sem, gm_sem, gm0_sem, gf_sem,
+    lperm, gl_send, gl_recv, gl_sum, gs_part, gs_recv, gs_all,
+    load_sem, ph_sem, g_sem, gm_sem, gm0_sem, gf_sem,
     fsend, frecv, lsend, lrecv, ssend, srecv, asend, arecv,
 ):
     me = lax.axis_index("seq")
@@ -419,9 +419,6 @@
 
     loop(0, CHUNKS, back_bulk)
 
-    def gp_store(c):
-        return pltpu.make_async_copy(gp_v.at[:, :, lanes(c)], gp_hbm.at[:, :, lanes(c)], store_sem.at[c])
-
     @pl.when(has_right)
     def _():
         gf_copy().wait_recv()
@@ -430,7 +427,6 @@
 
     def back_edge(c):
         back(c, ROWS - EDGE, EDGE)
-        gp_store(c).start()
 
     loop(0, CHUNKS, back_edge)
 
@@ -491,8 +487,6 @@
     def _():
         loop(0, SEQ, a_sent)
 
-    loop(0, CHUNKS, lambda c: gp_store(c).wait())
-
     def a_wait(p):
         @pl.when(p != my_piece)
         def _():
@@ -502,6 +496,14 @@
     for s in range(3):
         for c in range(CHUNKS):
             gs_out[s, :, c * LANES : (c + 1) * LANES] = gs_all[3 * c + s, 0:STAPS, :]
+
+
+def write_out(gp, gs, gl, gp_hbm, gs_hbm, gl_hbm, sems):
+    copies = [pltpu.make_async_copy(src, dst, sems.at[n]) for n, (src, dst) in enumerate(((gp, gp_hbm), (gs, gs_hbm), (gl, gl_hbm)))]
+    for copy in copies:
+        copy.start()
+    for copy in copies:
+        copy.wait()
 
 
 def on_device(projections, out_grad, short_filters, long_filter):
@@ -541,24 +543,31 @@
         vmem((PIECES, 8, LANES), F32),
         vmem((SEQ, 8, LANES), F32),
         vmem((PIECES, 8, LANES), F32),
-        vmem((3, ROWS, COLS), BF16),
-        dma((8,)), dma((CHUNKS,)), dma((2,)), dma((2, QUADS)), dma((2, QUADS)), dma((2,)), dma((2,)),
+        dma((8,)), dma((2,)), dma((2, QUADS)), dma((2, QUADS)), dma((2,)), dma((2,)),
         dma((SEQ,)), dma((SEQ,)), dma((SEQ,)), dma((SEQ,)), dma((PIECES,)), dma((SEQ,)), dma((SEQ,)), dma((SEQ,)),
     ]
     hbm = pl.BlockSpec(memory_space=pltpu.HBM)
     in_vmem = pl.BlockSpec(memory_space=pltpu.VMEM)
-    return pl.pallas_call(
+    operands = (projections, out_grad, short_filters, long_filter, jnp.asarray(forward), jnp.asarray(inverse))
+    results = pl.pallas_call(
         kernel,
         out_shape=(
-            jax.ShapeDtypeStruct(projections.shape, BF16),
-            jax.ShapeDtypeStruct(short_filters.shape, F32),
-            jax.ShapeDtypeStruct(long_filter.shape, F32),
+            pltpu.VMEM(projections.shape, BF16),
+            pltpu.VMEM(short_filters.shape, F32),
+            pltpu.VMEM(long_filter.shape, F32),
         ),
-        in_specs=[hbm] * 6,
-        out_specs=(hbm, in_vmem, in_vmem),
+        in_specs=[hbm] * len(operands),
+        out_specs=(in_vmem,) * 3,
         scratch_shapes=scratch,
         compiler_params=pltpu.CompilerParams(collective_id=0, has_side_effects=True, vmem_limit_bytes=50 << 20),
-    )(projections, out_grad, short_filters, long_filter, jnp.asarray(forward), jnp.asarray(inverse))
+    )(*[pltpu.with_memory_space_constraint(operand, pltpu.HBM) for operand in operands])
+    return pl.pallas_call(
+        write_out,
+        out_shape=tuple(jax.ShapeDtypeStruct(r.shape, r.dtype) for r in results),
+        in_specs=[in_vmem] * 3,
+        out_specs=(hbm,) * 3,
+        scratch_shapes=[dma((3,))],
+    )(*[pltpu.with_memory_space_constraint(result, pltpu.VMEM) for result in results])
 
 
 def solution(mesh):

time: 48.5 us -> 42.2 us (0.87)
  local copies, waits for them, and re-layouts: 6.99 us -> 0 us
  Pallas kernels: 40.5 us -> 41.5 us
    unnamed x13 -> x0, local copies, waits for them, and re-layouts: 6.99 us -> none
    pallas_call x1 -> x2, Pallas kernels: 40.5 us -> 41.5 us  [the longest x1 40.3 us: on_device(): pl.pallas_call(kernel, out_shape=(pltpu.VMEM(projections.shape, BF16), pl...]
where the time goes in v3:
time: 42.2 us; the launch traced here: 42.1 us
  Pallas kernels  41.5 us (98%)
  between operations  0.64 us (2%)
    pallas_call x1, Pallas kernels, on_device(): pl.pallas_call(kernel, out_shape=(pltpu.VMEM(projections.shape, BF16), pl...  40.3 us
    pallas_call x1, Pallas kernels, on_device(): pl.pallas_call(write_out, out_shape=tuple((jax.ShapeDtypeStruct(r.shape,...  1.19 us

profile of v3, /device:TPU:2, one launch (start us, length us, event | category | flops | bytes accessed | tf_op | source)
XLA Modules:
  0.0 42.1 jit_solution(18380275701958120867)
XLA Ops:
  0.6 40.3 %shard_map.85 = (bf16[3,256,1024]{2,1,0:T(8,128)(2,1)S(1)}, f32[3,7,1024]{2,1,0:T(8,128)S(1)}, f32[4,1024]{1,0:T(4,128)S(1)}) custom-call(bf16[3,256,1024]{2,1,0:T(8,128)(2,1)} %proj_hbm.1, bf16[256,1024]{1,0:T(8,128)(2,1)} %og_hbm.1, f32[3,7,1024]{2,1,0:T(8,128)} %sf_hbm.1, f32[4,1024]{1,0:T(4,128)} %lf_hbm.1, bf16[384,512]{1,0:T(8,128)(2,1)} %constant.4.clone.fw_hbm, ...), custom_call_target="tpu_custom_call" | custom-call | tf_op jit(solution)/shard_map/pallas_call | solution.py:552
  40.9 1.2 %shard_map.86 = (bf16[3,256,1024]{2,1,0:T(8,128)(2,1)}, f32[3,7,1024]{2,1,0:T(8,128)}, f32[4,1024]{1,0:T(4,128)}) custom-call(bf16[3,256,1024]{2,1,0:T(8,128)(2,1)S(1)} %get-tuple-element.6.gp, f32[3,7,1024]{2,1,0:T(8,128)S(1)} %get-tuple-element.7.gs, f32[4,1024]{1,0:T(4,128)S(1)} %get-tuple-element.8.gl), custom_call_target="tpu_custom_call" | custom-call | tf_op jit(solution)/shard_map/pallas_call | solution.py:564

commit v4 on v3

--- a/solution.py
+++ b/solution.py
@@ -24,11 +24,12 @@
 POINTS = ROWS + LTAPS
 HALF = POINTS // 2
 EDGE = 16
-PIECES = 3 * CHUNKS
+PIECES = 3 * QUADS
 ROW = 4
 COLUMN = 8
-FIRST_OWNER = 12
+FIRST_OWNER = 30
 HALO = STAPS - 1
+SHARE = LTAPS // ROW
 
 
 def transforms():
@@ -42,8 +43,10 @@
     prior = rows(np.arange(-LTAPS, 0))
     tap_order = np.arange(LTAPS).reshape(SEQ, OWN_TAPS).T.reshape(-1)
     taps = rows(tap_order)
-    forward = np.concatenate([own, prior, taps], axis=1).astype(ml_dtypes.bfloat16)
-    inverse = np.concatenate([own.T, taps.T], axis=0).astype(ml_dtypes.bfloat16)
+    own_rest = own - own.astype(ml_dtypes.bfloat16).astype(np.float64)
+    forward = np.concatenate([own, prior, taps, own_rest], axis=1).astype(ml_dtypes.bfloat16)
+    grad_order = np.arange(LTAPS).reshape(COLUMN, ROW, OWN_TAPS).transpose(1, 2, 0).reshape(-1)
+    inverse = np.concatenate([own.T, rows(grad_order).T], axis=0).astype(ml_dtypes.bfloat16)
     return forward, inverse
 
 
@@ -65,9 +68,9 @@
     pv, ov, sfv, lfv, fw, iv,
     xs, fs, fkv, gx, gmx, ph_stage, ph_send, ph_recv, gf_stage, gf_send, gf_recv,
     filt_a, filt_b, fperm, spec_g, spec_gm, spec_h, y1, y2,
-    lperm, gl_send, gl_recv, gl_sum, gs_part, gs_recv, gs_all,
+    lperm, gl_row_send, gl_row_recv, gl_send, gl_recv, gl_sum, gs_rows, gs_part, gs_recv, gs_all,
     load_sem, ph_sem, g_sem, gm_sem, gm0_sem, gf_sem,
-    fsend, frecv, lsend, lrecv, ssend, srecv, asend, arecv,
+    fsend, frecv, msend, mrecv, lsend, lrecv, ssend, srecv, asend, arecv,
 ):
     me = lax.axis_index("seq")
     right, left = lax.rem(me + 1, SEQ), lax.rem(me + SEQ - 1, SEQ)
@@ -225,6 +228,9 @@
 
     loop(0, CHUNKS, rest)
 
+    loop(1, ROW, lambda i: a1_copy(i).wait_recv())
+    loop(1, COLUMN, lambda i: a2_copy(i).start())
+
     @pl.when(has_left)
     def _():
         ph_copy().wait_recv()
@@ -251,20 +257,24 @@
     def _():
         gm0_copy().start()
 
-    loop(1, ROW, lambda i: a1_copy(i).wait_recv())
-    loop(1, COLUMN, lambda i: a2_copy(i).start())
-
     loads[6].wait()
     loads[7].wait()
 
     def own_spectra(q):
-        spec_g[:, wide(q)] = dot(fw[:, 0:ROWS], gx[LTAPS : LTAPS + ROWS, wide(q)])
-        spec_gm[:, wide(q)] = dot(fw[:, 0:ROWS], gmx[0:ROWS, wide(q)])
-
-    loop(0, QUADS, own_spectra)
+        for spec, values in ((spec_g, gx[LTAPS : LTAPS + ROWS, wide(q)]), (spec_gm, gmx[0:ROWS, wide(q)])):
+            spec[:, wide(q)] = dot(fw[:, 0:ROWS], values) + dot(fw[:, 2 * ROWS : 3 * ROWS], values)
+
+    loop(0, 2, own_spectra)
 
     loop(1, COLUMN, lambda i: b1_copy(i).wait_recv())
     loop(1, ROW, lambda i: b2_copy(i).start())
+
+    loop(2, QUADS, own_spectra)
+
+    def m_copy(q, i):
+        return remote(
+            gl_row_send.at[q, lax.rem(y + i, ROW)], gl_row_recv.at[q, i], msend.at[q, i], mrecv.at[q, i], in_row(i)
+        )
 
     for q in range(QUADS):
 
@@ -280,30 +290,27 @@
             oc, oi = spec_gm[re, cols], spec_gm[im, cols]
             y1[re, :] = (oc * gc + oi * gi).astype(BF16)
             y1[im, :] = (oi * gc - oc * gi).astype(BF16)
-        partial = dot(iv[ROWS:, :], y1[...])
-        for half in range(2):
-            for i in range(OWN_TAPS):
-                for first in range(0, SEQ, 8):
-                    rows = partial[SEQ * i + first : SEQ * i + first + 8, half * LANES : (half + 1) * LANES]
-                    lperm[half, pl.ds(16 * first + OWN_TAPS * q + i, 8, stride=16), :] = rows
-
-    def pack(d):
-        for half in range(2):
-            gl_send[d, :, half * LANES : (half + 1) * LANES] = lperm[half, pl.ds(pl.multiple_of(d * 16, 16), 16), :].astype(BF16)
-
-    loop(0, SEQ, pack)
+        partial = dot(iv[ROWS:, :], y1[...]).astype(BF16)
+        for row in range(ROW):
+            gl_row_send[q, row] = partial[SHARE * row : SHARE * (row + 1), :]
+        loop(1, ROW, lambda i: m_copy(q, i).start())
+
+    @pl.when(has_right)
+    def _():
+        gm0_copy().wait_recv()
+
+    for q in range(QUADS):
+
+        @pl.when(has_right)
+        def _():
+            gm_copy(q).wait_recv()
+
+        spec_gm[:, WIDE * q : WIDE * (q + 1)] -= dot(
+            fw[:, ROWS : ROWS + LTAPS], gmx[ROWS : ROWS + LTAPS, WIDE * q : WIDE * (q + 1)]
+        )
 
     loop(1, COLUMN, lambda i: a2_copy(i).wait_recv())
     loop(1, ROW, lambda i: b2_copy(i).wait_recv())
-
-    def l_copy(i):
-        return remote(gl_send.at[peer(i)], gl_recv.at[me], lsend.at[i], lrecv.at[me], peer(i))
-
-    def l_arrival(i):
-        return remote(gl_send.at[peer(i)], gl_recv.at[peer(i)], lsend.at[i], lrecv.at[peer(i)], peer(i))
-
-    loop(1, SEQ, lambda i: l_copy(i).start())
-    gl_recv[me] = gl_send[me]
 
     def unpack(d):
         rows = pl.ds(pl.multiple_of(d * 16, 16), 16)
@@ -322,11 +329,7 @@
             ]
             parts.append(jnp.concatenate(picked, axis=0).astype(BF16))
         taps = jnp.concatenate(parts, axis=1)
-        spec_h[:, WIDE * q : WIDE * (q + 1)] = dot(fw[:, ROWS + LTAPS :], taps) * (1.0 / HALF)
-
-    @pl.when(has_right)
-    def _():
-        gm0_copy().wait_recv()
+        spec_h[:, WIDE * q : WIDE * (q + 1)] = dot(fw[:, ROWS + LTAPS : 2 * ROWS], taps) * (1.0 / HALF)
 
     def gf_copy():
         return remote(gf_send, gf_recv, gf_sem.at[0], gf_sem.at[1], left)
@@ -348,7 +351,8 @@
     def a_arrival(p):
         return remote(gs_all.at[p], gs_all.at[p], asend.at[0], arecv.at[p], owner(p))
 
-    def short_grad(c):
+    def short_grad(q, half):
+        c = 2 * q + half
         for s in range(3):
             totals = [None] * STAPS
             for first in range(0, ROWS, 64):
@@ -356,21 +360,16 @@
                 for j in range(STAPS):
                     term = jnp.sum((grad * xs[s, c, pl.ds(EDGE + first - j, 64), :]).reshape(8, 8, LANES), axis=0)
                     totals[j] = term if totals[j] is None else totals[j] + term
-            rows = [jnp.sum(t, axis=0, keepdims=True) for t in totals] + [jnp.zeros((1, LANES), F32)]
-            gs_part[3 * c + s] = jnp.concatenate(rows, axis=0)
+            rows = jnp.concatenate([jnp.sum(t, axis=0, keepdims=True) for t in totals], axis=0)
+            start = STAPS * (3 * half + s)
+            gs_rows[q, start : start + STAPS, :] = rows
 
     def main(q):
-        @pl.when(has_right)
-        def _():
-            gm_copy(q).wait_recv()
-
-        later = dot(fw[:, ROWS : ROWS + LTAPS], gmx[ROWS : ROWS + LTAPS, wide(q)])
         for first in range(0, HALF, 64):
             re, im = pl.ds(first, 64), pl.ds(HALF + first, 64)
             gc, gi = spec_g[re, wide(q)], spec_g[im, wide(q)]
-            oc, oi = spec_gm[re, wide(q)], spec_gm[im, wide(q)]
+            mc, mi = spec_gm[re, wide(q)], spec_gm[im, wide(q)]
             hc, hi = spec_h[re, wide(q)], spec_h[im, wide(q)]
-            mc, mi = oc - later[first : first + 64], oi - later[HALF + first : HALF + first + 64]
             y1[re, :] = (gc * hc - gi * hi).astype(BF16)
             y1[im, :] = (gc * hi + gi * hc).astype(BF16)
             y2[re, :] = (mc * hc + mi * hi).astype(BF16)
@@ -384,18 +383,20 @@
             fs[1, c, 0:ROWS, :] = grad_gating[:, part] * fkv[1, c]
             fs[2, c, 0:ROWS, :] = grad_gating[:, part] * fkv[0, c]
 
+        gs_rows[q, 40:48, :] = jnp.zeros((8, LANES), F32)
         for half in range(2):
-            short_grad(2 * q + half)
-            for s in range(3):
-                piece = 3 * (2 * q + half) + s
-
-                @pl.when(piece != my_piece)
-                def _():
-                    s_copy(piece).start()
-
-                @pl.when(piece == my_piece)
-                def _():
-                    gs_recv[me] = gs_part[piece]
+            short_grad(q, half)
+        for k in range(3):
+            piece = 3 * q + k
+            gs_part[piece] = gs_rows[q, 16 * k : 16 * (k + 1), :].astype(BF16)
+
+            @pl.when(piece != my_piece)
+            def _():
+                s_copy(piece).start()
+
+            @pl.when(piece == my_piece)
+            def _():
+                gs_recv[me] = gs_part[piece]
 
     loop(0, QUADS, main)
 
@@ -404,6 +405,24 @@
     @pl.when(has_left)
     def _():
         gf_copy().start()
+
+    def l_copy(i):
+        return remote(gl_send.at[lax.rem(z + i, COLUMN)], gl_recv.at[i], lsend.at[i], lrecv.at[i], in_column(i))
+
+    for q in range(QUADS):
+        loop(1, ROW, lambda i: m_copy(q, i).wait_recv())
+        total = gl_row_send[q, y].astype(F32)
+        for i in range(1, ROW):
+            total = total + gl_row_recv[q, i].astype(F32)
+        for half in range(2):
+            for i in range(OWN_TAPS):
+                rows = total[COLUMN * i : COLUMN * (i + 1), half * LANES : (half + 1) * LANES]
+                lperm[half, pl.ds(OWN_TAPS * q + i, COLUMN, stride=16), :] = rows
+    for d in range(COLUMN):
+        for half in range(2):
+            gl_send[d, :, half * LANES : (half + 1) * LANES] = lperm[half, 16 * d : 16 * (d + 1), :].astype(BF16)
+    loop(1, COLUMN, lambda i: l_copy(i).start())
+    gl_recv[0] = gl_send[z]
 
     def back(c, first, count):
         for s in range(3):
@@ -438,15 +457,15 @@
     @pl.when(my_piece < PIECES)
     def _():
         loop(1, SEQ, lambda i: s_arrival(i).wait_recv())
-        total = gs_recv[0]
+        total = gs_recv[0].astype(F32)
         for d in range(1, SEQ):
-            total = total + gs_recv[d]
-        gs_all[my_piece] = total
+            total = total + gs_recv[d].astype(F32)
+        gs_all[my_piece] = total.astype(BF16)
         loop(0, SEQ, hand_out)
 
-    loop(1, SEQ, lambda i: l_arrival(i).wait_recv())
+    loop(1, COLUMN, lambda i: l_copy(i).wait_recv())
     total = gl_recv[0].astype(F32)
-    for d in range(1, SEQ):
+    for d in range(1, COLUMN):
         total = total + gl_recv[d].astype(F32)
     gl_sum[...] = total * (1.0 / HALF)
     for q in range(QUADS):
@@ -469,7 +488,9 @@
     for i in range(1, COLUMN):
         a2_copy(i).wait_send()
         b1_copy(i).wait_send()
-    loop(1, SEQ, lambda i: l_copy(i).wait_send())
+    loop(1, COLUMN, lambda i: l_copy(i).wait_send())
+    for q in range(QUADS):
+        loop(1, ROW, lambda i: m_copy(q, i).wait_send())
 
     def s_sent(p):
         @pl.when(p != my_piece)
@@ -493,9 +514,13 @@
             a_arrival(p).wait_recv()
 
     loop(0, PIECES, a_wait)
-    for s in range(3):
-        for c in range(CHUNKS):
-            gs_out[s, :, c * LANES : (c + 1) * LANES] = gs_all[3 * c + s, 0:STAPS, :]
+    for q in range(QUADS):
+        for k in range(3):
+            gs_rows[q, 16 * k : 16 * (k + 1), :] = gs_all[3 * q + k].astype(F32)
+        for half in range(2):
+            for s in range(3):
+                start, c = STAPS * (3 * half + s), 2 * q + half
+                gs_out[s, :, c * LANES : (c + 1) * LANES] = gs_rows[q, start : start + STAPS, :]
 
 
 def write_out(gp, gs, gl, gp_hbm, gs_hbm, gl_hbm, sems):
@@ -537,14 +562,17 @@
         vmem((POINTS, WIDE), BF16),
         vmem((POINTS, WIDE), BF16),
         vmem((2, SEQ * 16, LANES), F32),
-        vmem((SEQ, 16, WIDE), BF16),
-        vmem((SEQ, 16, WIDE), BF16),
+        vmem((QUADS, ROW, SHARE, WIDE), BF16),
+        vmem((QUADS, ROW, SHARE, WIDE), BF16),
+        vmem((COLUMN, 16, WIDE), BF16),
+        vmem((COLUMN, 16, WIDE), BF16),
         vmem((16, WIDE), F32),
-        vmem((PIECES, 8, LANES), F32),
-        vmem((SEQ, 8, LANES), F32),
-        vmem((PIECES, 8, LANES), F32),
+        vmem((QUADS, 48, LANES), F32),
+        vmem((PIECES, 16, LANES), BF16),
+        vmem((SEQ, 16, LANES), BF16),
+        vmem((PIECES, 16, LANES), BF16),
         dma((8,)), dma((2,)), dma((2, QUADS)), dma((2, QUADS)), dma((2,)), dma((2,)),
-        dma((SEQ,)), dma((SEQ,)), dma((SEQ,)), dma((SEQ,)), dma((PIECES,)), dma((SEQ,)), dma((SEQ,)), dma((SEQ,)),
+        dma((SEQ,)), dma((SEQ,)), dma((QUADS, ROW)), dma((QUADS, ROW)), dma((COLUMN,)), dma((COLUMN,)), dma((PIECES,)), dma((SEQ,)), dma((SEQ,)), dma((SEQ,)),
     ]
     hbm = pl.BlockSpec(memory_space=pltpu.HBM)
     in_vmem = pl.BlockSpec(memory_space=pltpu.VMEM)

time: 42.2 us -> 39.4 us (0.934)
  Pallas kernels: 41.5 us -> 38.6 us
    pallas_call x1, Pallas kernels: 40.3 us -> 37.4 us  [on_device(): pl.pallas_call(kernel, out_shape=(pltpu.VMEM(projections.shape, BF16), pl...]
where the time goes in v4:
time: 39.4 us; the launch traced here: 39.3 us
  Pallas kernels  38.6 us (98%)
  between operations  0.64 us (2%)
    pallas_call x1, Pallas kernels, on_device(): pl.pallas_call(kernel, out_shape=(pltpu.VMEM(projections.shape, BF16), pl...  37.4 us
    pallas_call x1, Pallas kernels, on_device(): pl.pallas_call(write_out, out_shape=tuple((jax.ShapeDtypeStruct(r.shape,...  1.19 us

profile of v4, /device:TPU:2, one launch (start us, length us, event | category | flops | bytes accessed | tf_op | source)
XLA Modules:
  0.0 39.3 jit_solution(10016037493129006352)
XLA Ops:
  0.6 37.4 %shard_map.85 = (bf16[3,256,1024]{2,1,0:T(8,128)(2,1)S(1)}, f32[3,7,1024]{2,1,0:T(8,128)S(1)}, f32[4,1024]{1,0:T(4,128)S(1)}) custom-call(bf16[3,256,1024]{2,1,0:T(8,128)(2,1)} %proj_hbm.1, bf16[256,1024]{1,0:T(8,128)(2,1)} %og_hbm.1, f32[3,7,1024]{2,1,0:T(8,128)} %sf_hbm.1, f32[4,1024]{1,0:T(4,128)} %lf_hbm.1, bf16[384,768]{1,0:T(8,128)(2,1)} %constant.4.clone.fw_hbm, ...), custom_call_target="tpu_custom_call" | custom-call | tf_op jit(solution)/shard_map/pallas_call | solution.py:580
  38.1 1.2 %shard_map.86 = (bf16[3,256,1024]{2,1,0:T(8,128)(2,1)}, f32[3,7,1024]{2,1,0:T(8,128)}, f32[4,1024]{1,0:T(4,128)}) custom-call(bf16[3,256,1024]{2,1,0:T(8,128)(2,1)S(1)} %get-tuple-element.6.gp, f32[3,7,1024]{2,1,0:T(8,128)S(1)} %get-tuple-element.7.gs, f32[4,1024]{1,0:T(4,128)S(1)} %get-tuple-element.8.gl), custom_call_target="tpu_custom_call" | custom-call | tf_op jit(solution)/shard_map/pallas_call | solution.py:592

commit v5 on v4

--- a/solution.py
+++ b/solution.py
@@ -264,12 +264,10 @@
         for spec, values in ((spec_g, gx[LTAPS : LTAPS + ROWS, wide(q)]), (spec_gm, gmx[0:ROWS, wide(q)])):
             spec[:, wide(q)] = dot(fw[:, 0:ROWS], values) + dot(fw[:, 2 * ROWS : 3 * ROWS], values)
 
-    loop(0, 2, own_spectra)
-
     loop(1, COLUMN, lambda i: b1_copy(i).wait_recv())
     loop(1, ROW, lambda i: b2_copy(i).start())
 
-    loop(2, QUADS, own_spectra)
+    loop(0, QUADS, own_spectra)
 
     def m_copy(q, i):
         return remote(
@@ -312,13 +310,11 @@
     loop(1, COLUMN, lambda i: a2_copy(i).wait_recv())
     loop(1, ROW, lambda i: b2_copy(i).wait_recv())
 
-    def unpack(d):
-        rows = pl.ds(pl.multiple_of(d * 16, 16), 16)
-        dz, dy = lax.div(d, ROW), lax.rem(d, ROW)
-        fperm[0, rows, :] = filt_a[dz, dy].astype(F32)
-        fperm[1, rows, :] = filt_b[dy, dz].astype(F32)
-
-    loop(0, SEQ, unpack)
+    for d in range(SEQ):
+        dz, dy = divmod(d, ROW)
+        fperm[0, 16 * d : 16 * (d + 1), :] = filt_a[dz, dy].astype(F32)
+        fperm[1, 16 * d : 16 * (d + 1), :] = filt_b[dy, dz].astype(F32)
+
     for q in range(QUADS):
         parts = []
         for half in range(2):
@@ -383,9 +379,12 @@
             fs[1, c, 0:ROWS, :] = grad_gating[:, part] * fkv[1, c]
             fs[2, c, 0:ROWS, :] = grad_gating[:, part] * fkv[0, c]
 
+    def shorts(q):
         gs_rows[q, 40:48, :] = jnp.zeros((8, LANES), F32)
         for half in range(2):
             short_grad(q, half)
+
+    def give(q):
         for k in range(3):
             piece = 3 * q + k
             gs_part[piece] = gs_rows[q, 16 * k : 16 * (k + 1), :].astype(BF16)
@@ -398,7 +397,13 @@
             def _():
                 gs_recv[me] = gs_part[piece]
 
-    loop(0, QUADS, main)
+    main(0)
+    for q in range(1, QUADS):
+        main(q)
+        shorts(q - 1)
+        give(q - 1)
+    shorts(QUADS - 1)
+    give(QUADS - 1)
 
     fold(gf_stage, fs, 0, gf_send)
 

time: 39.4 us -> 38.4 us (0.975)
  Pallas kernels: 38.6 us -> 37.7 us
    pallas_call x1, Pallas kernels: 37.4 us -> 36.5 us  [on_device(): pl.pallas_call(kernel, out_shape=(pltpu.VMEM(projections.shape, BF16), pl...]
where the time goes in v5:
time: 38.4 us; the launch traced here: 38.3 us
  Pallas kernels  37.7 us (98%)
  between operations  0.64 us (2%)
    pallas_call x1, Pallas kernels, on_device(): pl.pallas_call(kernel, out_shape=(pltpu.VMEM(projections.shape, BF16), pl...  36.5 us
    pallas_call x1, Pallas kernels, on_device(): pl.pallas_call(write_out, out_shape=tuple((jax.ShapeDtypeStruct(r.shape,...  1.19 us

profile of v5, /device:TPU:2, one launch (start us, length us, event | category | flops | bytes accessed | tf_op | source)
XLA Modules:
  0.0 38.3 jit_solution(9316738992085275921)
XLA Ops:
  0.6 36.5 %shard_map.85 = (bf16[3,256,1024]{2,1,0:T(8,128)(2,1)S(1)}, f32[3,7,1024]{2,1,0:T(8,128)S(1)}, f32[4,1024]{1,0:T(4,128)S(1)}) custom-call(bf16[3,256,1024]{2,1,0:T(8,128)(2,1)} %proj_hbm.1, bf16[256,1024]{1,0:T(8,128)(2,1)} %og_hbm.1, f32[3,7,1024]{2,1,0:T(8,128)} %sf_hbm.1, f32[4,1024]{1,0:T(4,128)} %lf_hbm.1, bf16[384,768]{1,0:T(8,128)(2,1)} %constant.4.clone.fw_hbm, ...), custom_call_target="tpu_custom_call" | custom-call | tf_op jit(solution)/shard_map/pallas_call | solution.py:585
  37.2 1.2 %shard_map.86 = (bf16[3,256,1024]{2,1,0:T(8,128)(2,1)}, f32[3,7,1024]{2,1,0:T(8,128)}, f32[4,1024]{1,0:T(4,128)}) custom-call(bf16[3,256,1024]{2,1,0:T(8,128)(2,1)S(1)} %get-tuple-element.6.gp, f32[3,7,1024]{2,1,0:T(8,128)S(1)} %get-tuple-element.7.gs, f32[4,1024]{1,0:T(4,128)S(1)} %get-tuple-element.8.gl), custom_call_target="tpu_custom_call" | custom-call | tf_op jit(solution)/shard_map/pallas_call | solution.py:597

commit v6 on v5

--- a/solution.py
+++ b/solution.py
@@ -166,11 +166,11 @@
             stage[c, 12:16, :] = source[2, c, first : first + 4, :]
             stage[CHUNKS, 2 * c : 2 * c + 2, :] = source[2, c, first + 4 : first + 6, :]
         for c in range(CHUNKS + 1):
-            packed[:, LANES * c : LANES * (c + 1)] = stage[c].astype(BF16)
+            packed[:, LANES * c : LANES * (c + 1)] = stage[c, 0:EDGE, :].astype(BF16)
 
     def unfold(packed, stage, target, first):
         for c in range(CHUNKS + 1):
-            stage[c] = packed[:, LANES * c : LANES * (c + 1)].astype(F32)
+            stage[c, 0:EDGE, :] = packed[:, LANES * c : LANES * (c + 1)].astype(F32)
         for c in range(CHUNKS):
             target[0, c, first : first + 6, :] = stage[c, 0:6, :]
             target[1, c, first : first + 6, :] = stage[c, 6:12, :]
@@ -472,7 +472,7 @@
     total = gl_recv[0].astype(F32)
     for d in range(1, COLUMN):
         total = total + gl_recv[d].astype(F32)
-    gl_sum[...] = total * (1.0 / HALF)
+    gl_sum[0:16, :] = total * (1.0 / HALF)
     for q in range(QUADS):
         gl_out[:, WIDE * q : WIDE * (q + 1)] = gl_sum[OWN_TAPS * q : OWN_TAPS * (q + 1), :]
 
@@ -552,27 +552,27 @@
         vmem((2, CHUNKS, ROWS, LANES), F32),
         vmem((LTAPS + ROWS, COLS), BF16),
         vmem((ROWS + LTAPS, COLS), BF16),
-        vmem((CHUNKS + 1, EDGE, LANES), F32),
+        vmem((CHUNKS + 1, EDGE + 8, LANES), F32),
         vmem((EDGE, COLS + LANES), BF16),
         vmem((EDGE, COLS + LANES), BF16),
-        vmem((CHUNKS + 1, EDGE, LANES), F32),
+        vmem((CHUNKS + 1, EDGE + 8, LANES), F32),
         vmem((EDGE, COLS + LANES), BF16),
         vmem((EDGE, COLS + LANES), BF16),
         vmem((COLUMN, ROW, 16, LANES), BF16),
         vmem((ROW, COLUMN, 16, LANES), BF16),
-        vmem((2, SEQ * 16, LANES), F32),
+        vmem((2, SEQ * 16 + LANES, LANES), F32),
         vmem((POINTS, COLS), F32),
         vmem((POINTS, COLS), F32),
         vmem((POINTS, COLS), F32),
         vmem((POINTS, WIDE), BF16),
         vmem((POINTS, WIDE), BF16),
-        vmem((2, SEQ * 16, LANES), F32),
+        vmem((2, SEQ * 16 + LANES, LANES), F32),
         vmem((QUADS, ROW, SHARE, WIDE), BF16),
         vmem((QUADS, ROW, SHARE, WIDE), BF16),
         vmem((COLUMN, 16, WIDE), BF16),
         vmem((COLUMN, 16, WIDE), BF16),
-        vmem((16, WIDE), F32),
-        vmem((QUADS, 48, LANES), F32),
+        vmem((24, WIDE), F32),
+        vmem((QUADS, 56, LANES), F32),
         vmem((PIECES, 16, LANES), BF16),
         vmem((SEQ, 16, LANES), BF16),
         vmem((PIECES, 16, LANES), BF16),

time: 38.4 us -> 38.5 us (level)
  no operation moved by 1% of the time
where the time goes in v6:
time: 38.5 us; the launch traced here: 38.4 us
  Pallas kernels  37.7 us (98%)
  between operations  0.64 us (2%)
    pallas_call x1, Pallas kernels, on_device(): pl.pallas_call(kernel, out_shape=(pltpu.VMEM(projections.shape, BF16), pl...  36.5 us
    pallas_call x1, Pallas kernels, on_device(): pl.pallas_call(write_out, out_shape=tuple((jax.ShapeDtypeStruct(r.shape,...  1.19 us

profile of v6, /device:TPU:2, one launch (start us, length us, event | category | flops | bytes accessed | tf_op | source)
XLA Modules:
  0.0 38.4 jit_solution(8089210028187992084)
XLA Ops:
  0.6 36.5 %shard_map.85 = (bf16[3,256,1024]{2,1,0:T(8,128)(2,1)S(1)}, f32[3,7,1024]{2,1,0:T(8,128)S(1)}, f32[4,1024]{1,0:T(4,128)S(1)}) custom-call(bf16[3,256,1024]{2,1,0:T(8,128)(2,1)} %proj_hbm.1, bf16[256,1024]{1,0:T(8,128)(2,1)} %og_hbm.1, f32[3,7,1024]{2,1,0:T(8,128)} %sf_hbm.1, f32[4,1024]{1,0:T(4,128)} %lf_hbm.1, bf16[384,768]{1,0:T(8,128)(2,1)} %constant.4.clone.fw_hbm, ...), custom_call_target="tpu_custom_call" | custom-call | tf_op jit(solution)/shard_map/pallas_call | solution.py:585
  37.2 1.2 %shard_map.86 = (bf16[3,256,1024]{2,1,0:T(8,128)(2,1)}, f32[3,7,1024]{2,1,0:T(8,128)}, f32[4,1024]{1,0:T(4,128)}) custom-call(bf16[3,256,1024]{2,1,0:T(8,128)(2,1)S(1)} %get-tuple-element.6.gp, f32[3,7,1024]{2,1,0:T(8,128)S(1)} %get-tuple-element.7.gs, f32[4,1024]{1,0:T(4,128)S(1)} %get-tuple-element.8.gl), custom_call_target="tpu_custom_call" | custom-call | tf_op jit(solution)/shard_map/pallas_call | solution.py:597
